TPU v7x, 32 devices: a whole 2x2x4 slice. The times are simulated.
32 devices in a mesh: src: 4 (over y, core), tile: 8 (over z, x).
Axes of the slice: x: 2, y: 2, z: 4, core: 2. Of those that a mesh axis runs over, the one named last changes fastest.
Arguments:
- mask: bfloat16 [256, 4096], P('src', 'tile'), may hold values from -6 to 6
- target: bfloat16 [256, 4096], P('src', 'tile'), may hold values from 0 to 1
- start_block: float32 [2, 24, 128, 128], replicated, may hold values from -6 to 6
- zernike: float32 [8, 37], replicated, may hold values from -0.3 to 0.3
- source_points: int32 [512, 2], replicated, may hold values from -24 to 24
- source_weight: float32 [512], replicated, may hold values from 0.25 to 1
- tile_slit: int32 [16], P('tile'), may hold values from 0 to 7
Outputs:
- resist: bfloat16 [256, 4096], P('src', 'tile')
- mask_grad: bfloat16 [256, 4096], P('src', 'tile')
All inputs are finite; a program needn't handle non-finite values.
Results may differ from a plain program's by a relative error of at most 0.024.
Values may be sent and summed in bfloat16 or wider, within the bound.
A program may use at most 128 MiB of HBM per device.

v0:
```python
import math

import jax
import jax.numpy as jnp
from jax import lax
from jax.sharding import PartitionSpec as P

KB = 128
NR = 24
NZ = 37
RAD = 40
SHIFT = 24
HALO = 64
ITERS = 4
TS = 256


STEEPNESS = 4.0
THRESHOLD = 0.5
RIDGE_SHARE = 0.001
EXACT_MODE = lax.Precision.HIGHEST


def with_halo(cells, sides, width):
    for axis, dim in sides:
        count = lax.axis_size(axis)
        ends = count - 1
        head = lax.slice_in_dim(cells, 0, width, axis=dim)
        tail = lax.slice_in_dim(cells, cells.shape[dim] - width, cells.shape[dim], axis=dim)
        cells = jnp.concatenate(
            [
                lax.ppermute(tail, axis, [(i, (i + 1) % count) for i in range(ends)]),
                cells,
                lax.ppermute(head, axis, [((i + 1) % count, i) for i in range(ends)]),
            ],
            axis=dim,
        )
    return cells


def noll_terms(term_count):
    listing = []
    degree = 0
    while len(listing) < term_count:
        for azimuth in range(degree % 2, degree + 1, 2):
            if azimuth == 0:
                listing.append((degree, 0, 0))
            else:
                for repeat in range(2):
                    number = len(listing) + 1
                    listing.append((degree, azimuth, 2 if number % 2 == 0 else 1))
        degree += 1
    return listing[:term_count]


def radial_terms(degree, azimuth):
    powers = []
    for counter in range((degree - azimuth) // 2 + 1):
        factor = (
            (-1) ** counter
            * math.factorial(degree - counter)
            / (
                math.factorial(counter)
                * math.factorial((degree + azimuth) // 2 - counter)
                * math.factorial((degree - azimuth) // 2 - counter)
            )
        )
        powers.append((degree - 2 * counter, factor))
    return powers


def pupil_grid(coefficients):
    extent = KB + 2 * SHIFT
    coords = jnp.arange(extent, dtype=jnp.int32) - (KB // 2 + SHIFT)
    row_coord = coords[:, None]
    col_coord = coords[None, :]
    radius_sq = row_coord * row_coord + col_coord * col_coord
    inside = (radius_sq <= RAD * RAD).astype(jnp.float32)
    radius = jnp.sqrt(radius_sq.astype(jnp.float32)) / RAD
    azimuth_angle = jnp.arctan2(
        col_coord.astype(jnp.float32) + 0.0 * radius, row_coord.astype(jnp.float32) + 0.0 * radius
    )
    aberration = jnp.zeros((extent, extent), jnp.float32)
    for position, (degree, azimuth, parity) in enumerate(noll_terms(NZ)):
        radial = jnp.zeros((extent, extent), jnp.float32)
        for exponent, factor in radial_terms(degree, azimuth):
            radial = radial + factor * radius**exponent
        if azimuth == 0:
            profile = math.sqrt(degree + 1.0) * radial
        elif parity == 2:
            profile = math.sqrt(2.0 * degree + 2.0) * radial * jnp.cos(azimuth * azimuth_angle)
        else:
            profile = math.sqrt(2.0 * degree + 2.0) * radial * jnp.sin(azimuth * azimuth_angle)
        aberration = aberration + coefficients[position] * profile
    phase_angle = 2.0 * math.pi * aberration
    return jnp.stack([inside * jnp.cos(phase_angle), inside * jnp.sin(phase_angle)])


def source_windows(pupil_values, offsets, row_start, row_total):

    def single(offset):
        return lax.dynamic_slice(
            pupil_values,
            (jnp.zeros((), jnp.int32), offset[0] + SHIFT + row_start, offset[1] + SHIFT),
            (2, row_total, KB),
        )

    windowed = jax.vmap(single)(offsets)
    return windowed.reshape(offsets.shape[0], 2 * row_total * KB)


def pupil_products(windows, kernel_block):
    real_pairs = jnp.concatenate([kernel_block[0], kernel_block[1]], axis=1)
    imag_pairs = jnp.concatenate([kernel_block[1], -kernel_block[0]], axis=1)
    stacked = jnp.concatenate([real_pairs, imag_pairs], axis=0)
    return jnp.einsum("sf,kf->sk", windows, stacked, precision=EXACT_MODE)


def spread_terms(windows, products):
    spread = jnp.einsum("sk,sf->kf", products, windows, precision=EXACT_MODE)
    half_width = spread.shape[1] // 2
    image_re = spread[:NR, :half_width] - spread[NR:, half_width:]
    image_im = spread[NR:, :half_width] + spread[:NR, half_width:]
    return jnp.stack([image_re, image_im])


def inner_products(left_block, right_block):
    return jnp.einsum("zkf,zlf->kl", left_block, right_block, precision=EXACT_MODE)


def orthonormal(applied, gram_matrix):
    shift_term = RIDGE_SHARE * jnp.trace(gram_matrix) / NR + 1e-06
    factor = jnp.linalg.cholesky(gram_matrix + shift_term * jnp.eye(NR, dtype=jnp.float32))
    inverse = jax.scipy.linalg.solve_triangular(factor, jnp.eye(NR, dtype=jnp.float32), lower=True)
    return jnp.einsum("kl,zlf->zkf", inverse, applied, precision=EXACT_MODE)


def synthesize(coefficients, source_points, source_weight, start_block, group_rank, group_size):
    pupil_values = pupil_grid(coefficients)
    weighting = source_weight / (math.pi * RAD * RAD * jnp.sum(source_weight))
    row_total = KB
    per_device = source_points.shape[0] // group_size
    my_points = lax.dynamic_slice_in_dim(source_points, group_rank * per_device, per_device, 0)
    my_weights = lax.dynamic_slice_in_dim(weighting, group_rank * per_device, per_device, 0)
    windows = source_windows(pupil_values, my_points, 0, KB)
    kernel_block = start_block.reshape(2, NR, KB * KB)
    for iteration in range(ITERS + 1):
        products = pupil_products(windows, kernel_block) * my_weights[:, None]
        applied = lax.psum(spread_terms(windows, products).astype(jnp.bfloat16), "src").astype(
            jnp.float32
        )
        if iteration < ITERS:
            kernel_block = orthonormal(applied, inner_products(applied, applied))
    mixing = inner_products(kernel_block, applied)
    mixing = (0.5 * (mixing + mixing.T)).astype(jnp.bfloat16)
    return (kernel_block.reshape(2, NR, row_total, KB).astype(jnp.bfloat16), mixing)


def gather_rows(kernel_parts):
    return lax.all_gather(kernel_parts, "src", axis=3, tiled=True)


def phase_table(positions, period):
    frequency = jnp.arange(KB, dtype=jnp.int32) - KB // 2
    residue = jnp.mod(positions[:, None] * frequency[None, :], period)
    angles = 2.0 * math.pi / period * residue.astype(jnp.float32)
    return (jnp.cos(angles).astype(jnp.bfloat16), jnp.sin(angles).astype(jnp.bfloat16))


def row_phase_table(positions):
    cosine_table, sine_table = phase_table(positions, TS)
    return jnp.concatenate([cosine_table, sine_table], axis=1)


def column_tables():
    patch_width = TS + 2 * HALO
    cosine_table, sine_table = phase_table(jnp.arange(patch_width, dtype=jnp.int32), patch_width)
    column_forward = jnp.concatenate([cosine_table, -sine_table], axis=1)
    inner_cos = cosine_table[HALO : HALO + TS]
    inner_sin = sine_table[HALO : HALO + TS]
    column_inverse = jnp.concatenate([inner_cos, -inner_sin], axis=1)
    column_adjoint = jnp.concatenate([inner_cos, inner_sin], axis=1)
    return (column_forward, column_inverse, column_adjoint)


def tile_response(
    spectrum_re, spectrum_im, kernel, mixing, goal_tile, row_table, column_inverse, column_adjoint
):
    kernel_re = kernel[0].astype(jnp.float32)
    kernel_im = kernel[1].astype(jnp.float32)
    product_re = (kernel_re * spectrum_re + kernel_im * spectrum_im).astype(jnp.bfloat16)
    product_im = (kernel_re * spectrum_im - kernel_im * spectrum_re).astype(jnp.bfloat16)
    blocks = jnp.concatenate(
        [
            jnp.concatenate([product_re, product_im], axis=2),
            jnp.concatenate([-product_im, product_re], axis=2),
        ],
        axis=1,
    )
    rows_mixed = jnp.einsum(
        "xc,kcd->kxd", row_table, blocks, preferred_element_type=jnp.float32
    ).astype(jnp.bfloat16)
    fields = jnp.einsum(
        "kxc,yc->kxy", rows_mixed, column_inverse, preferred_element_type=jnp.float32
    )
    mixed_fields = jnp.einsum(
        "kl,lxy->kxy", mixing.astype(jnp.float32), fields, precision=EXACT_MODE
    )
    intensity = jnp.sum(fields * mixed_fields, axis=0)
    resist = jax.nn.sigmoid(STEEPNESS * (intensity - THRESHOLD))
    resist_slope = (
        2.0 * (resist - goal_tile.astype(jnp.float32)) * STEEPNESS * resist * (1.0 - resist)
    )
    field_grad = (2.0 * mixed_fields * resist_slope[None]).astype(jnp.bfloat16)
    adjoint_cols = jnp.einsum(
        "kxy,yc->kxc", field_grad, column_adjoint, preferred_element_type=jnp.float32
    ).astype(jnp.bfloat16)
    adjoint_rows = jnp.einsum(
        "xc,kxd->kcd", row_table, adjoint_cols, preferred_element_type=jnp.float32
    )
    turned_re = adjoint_rows[:, :KB, :KB] - adjoint_rows[:, KB:, KB:]
    turned_im = adjoint_rows[:, :KB, KB:] + adjoint_rows[:, KB:, :KB]
    grad_re = jnp.sum(kernel_re * turned_re + kernel_im * turned_im, axis=0)
    grad_im = jnp.sum(kernel_im * turned_re - kernel_re * turned_im, axis=0)
    return (resist.astype(jnp.bfloat16), grad_re, grad_im)


def patch_gradient(grad_re, grad_im, spectrum_scale, row_table, column_forward):
    back_re = (spectrum_scale * grad_re).astype(jnp.bfloat16)
    back_im = (spectrum_scale * grad_im).astype(jnp.bfloat16)
    back_block = jnp.concatenate(
        [jnp.concatenate([back_re, back_im], axis=1), jnp.concatenate([-back_im, back_re], axis=1)],
        axis=0,
    )
    back_rows = jnp.dot(row_table, back_block, preferred_element_type=jnp.float32).astype(
        jnp.bfloat16
    )
    return jnp.einsum("xc,yc->xy", back_rows, column_forward, preferred_element_type=jnp.float32)


def on_device(mask, target, start_block, zernike, source_points, source_weight, tile_slit):
    group_size = lax.axis_size("src")
    group_rank = lax.axis_index("src")
    rows_here = mask.shape[0]
    width_here = mask.shape[1]
    tiles_here = tile_slit.shape[0]
    kernel_block, mixing = synthesize(
        zernike[lax.axis_index("tile")],
        source_points,
        source_weight,
        start_block,
        group_rank,
        group_size,
    )
    row_part = KB // group_size
    kernel_block = lax.dynamic_slice_in_dim(kernel_block, group_rank * row_part, row_part, 2)
    stored_kernels = jnp.zeros((tiles_here,) + kernel_block.shape, jnp.bfloat16)
    stored_mixing = jnp.zeros((tiles_here, NR, NR), jnp.bfloat16)
    received_kernels = lax.all_gather(kernel_block[None], "tile", axis=0, tiled=True)
    received_mixing = lax.all_gather(mixing[None], "tile", axis=0, tiled=True)
    available = received_kernels.shape[0]
    matches = (tile_slit >= 0) & (tile_slit < available)
    clipped = jnp.clip(tile_slit, 0, available - 1)
    taken_kernels = jnp.take(received_kernels, clipped, axis=0)
    taken_mixing = jnp.take(received_mixing, clipped, axis=0)
    kernel_parts = jnp.where(matches[:, None, None, None, None], taken_kernels, stored_kernels)
    mixings = jnp.where(matches[:, None, None], taken_mixing, stored_mixing)
    kernels = gather_rows(kernel_parts)
    extended = with_halo(mask, (("tile", 1),), HALO)
    patch_width = TS + 2 * HALO
    spectrum_scale = 1.0 / math.sqrt(TS * patch_width)
    row_table = row_phase_table(group_rank * rows_here + jnp.arange(rows_here, dtype=jnp.int32))
    column_forward, column_inverse, column_adjoint = column_tables()
    patches = jnp.stack(
        [extended[:, counter * TS : counter * TS + patch_width] for counter in range(tiles_here)]
    )
    columns = jnp.einsum(
        "jxy,yc->jxc", patches, column_forward, preferred_element_type=jnp.float32
    ).astype(jnp.bfloat16)
    row_sums = jnp.einsum("xc,jxd->jcd", row_table, columns, preferred_element_type=jnp.float32)
    partial_re = row_sums[:, :KB, :KB] + row_sums[:, KB:, KB:]
    partial_im = row_sums[:, :KB, KB:] - row_sums[:, KB:, :KB]
    summed_re, summed_im = (
        lax.psum(partial_re.astype(jnp.bfloat16), "src").astype(jnp.float32),
        lax.psum(partial_im.astype(jnp.bfloat16), "src").astype(jnp.float32),
    )
    spectrum_re = spectrum_scale * summed_re
    spectrum_im = spectrum_scale * summed_im
    resist_list = []
    grad_re_list = []
    grad_im_list = []
    for counter in range(tiles_here):
        goal_tile = target[:, counter * TS : (counter + 1) * TS]
        resist_tile, grad_re, grad_im = tile_response(
            spectrum_re[counter],
            spectrum_im[counter],
            kernels[counter],
            mixings[counter],
            goal_tile,
            row_table,
            column_inverse,
            column_adjoint,
        )
        resist_list.append(resist_tile)
        grad_re_list.append(grad_re)
        grad_im_list.append(grad_im)
    total_re, total_im = (
        lax.psum(jnp.stack(grad_re_list).astype(jnp.bfloat16), "src").astype(jnp.float32),
        lax.psum(jnp.stack(grad_im_list).astype(jnp.bfloat16), "src").astype(jnp.float32),
    )
    accumulated = jnp.zeros((rows_here, width_here + 2 * HALO), jnp.float32)
    for counter in range(tiles_here):
        patch_grad = patch_gradient(
            total_re[counter], total_im[counter], spectrum_scale, row_table, column_forward
        )
        accumulated = accumulated.at[:, counter * TS : counter * TS + patch_width].add(patch_grad)
    rim_cols = jnp.concatenate([accumulated[:, :HALO], accumulated[:, width_here + HALO :]], axis=1)
    beside_all = with_halo(rim_cols.astype(jnp.bfloat16), (("tile", 1),), HALO).astype(
        rim_cols.dtype
    )
    from_left = beside_all[:, :HALO]
    from_right = beside_all[:, 3 * HALO :]
    inner_part = accumulated[:, HALO : HALO + width_here]
    inner_part = (
        inner_part
        + jnp.pad(from_left, ((0, 0), (0, width_here - HALO)))
        + jnp.pad(from_right, ((0, 0), (width_here - HALO, 0)))
    )
    resist = jnp.concatenate(resist_list, axis=1)
    return (resist, inner_part.astype(jnp.bfloat16))


def solution(mesh):
    placed = (P("src", "tile"), P("src", "tile"), P(), P(), P(), P(), P("tile"))
    return jax.shard_map(
        on_device,
        mesh=mesh,
        in_specs=placed,
        out_specs=(P("src", "tile"), P("src", "tile")),
        check_vma=False,
    )
```

profile of v0, /device:TPU:0, one launch (start us, length us, event | category | flops | bytes accessed | tf_op | source)
XLA Modules:
  0.0 1076.2 jit_solution(10778963466427666678)
XLA Ops:
  11.9 27.4 %fusion.178 = (f32[1,176,176]{2,1,0:T(8,128)S(1)}, f32[1,176,176]{2,1,0:T(8,128)S(1)}) fusion(s32[176]{0:T(256)S(1)} %get-tuple-element.170, f32[]{:T(128)} %bitcast.36, f32[]{:T(128)} %bitcast.35, f32[]{:T(128)} %bitcast.34, f32[]{:T(128)} %bitcast.33, f32[]{:T(128)} %bitcast.32, f32[]{:T(128)} %bitcast.31, f32[]{:T(128)} %bitcast.30, f32[]{:T(128)} %bitcast.29, ...), kind=kLoop, calls=%fused_computation.232 | loop fusion | flops 6164224 | bytes 249364 | tf_op jit(solution)/shard_map/mul | solution.py:96
  40.1 328.4 %while.3 = (s32[]{:T(128)}, f32[2,176,176]{2,1,0:T(8,128)S(1)}, s32[128,3]{0,1:T(4,128)S(1)}, f32[128,2,128,128]{3,2,1,0:T(8,128)}, s32[]{:T(128)}) while((s32[]{:T(128)}, f32[2,176,176]{2,1,0:T(8,128)S(1)}, s32[128,3]{0,1:T(4,128)S(1)}, f32[128,2,128,128]{3,2,1,0:T(8,128)}, s32[]{:T(128)}) %tuple.115), condition=%wide.while_cond.2, body=%wide.while_body.2.sunk | while | flops 2 | bytes 263785 | solution.py:102
  374.8 31.1 %fusion.131 = f32[128,48]{0,1:T(8,128)S(1)} fusion(f32[24,16384]{1,0:T(8,128)S(1)} %fusion.406, f32[24,16384]{1,0:T(8,128)S(1)} %get-tuple-element.171, f32[24,16384]{1,0:T(8,128)S(1)} %get-tuple-element.172, f32[16,8,256,128]{3,2,1,0:T(8,128)} %bitcast.370, f32[128]{0:T(128)S(1)} %dynamic_slice.14), kind=kOutput, calls=%fused_computation.186 | convolution fusion | flops 2420643840 | bytes 21520896 | tf_op jit(solution)/shard_map/sf,kf->sk/dot_general | solution.py:116
  405.8 24.2 %fusion.16 = f32[48,32768]{1,0:T(8,128)S(1)} fusion(f32[128,48]{0,1:T(8,128)S(1)} %fusion.131, f32[16,8,256,128]{3,2,1,0:T(8,128)} %bitcast.371), kind=kOutput, calls=%fused_computation.24 | convolution fusion | flops 2415919104 | bytes 23093248 | tf_op jit(solution)/shard_map/sk,sf->kf/dot_general | solution.py:120
  431.7 45.6 %all-reduce.12.cloned.1.call-done = bf16[2,24,16384]{2,1,0:T(8,128)(2,1)} async-done(((bf16[2,24,16384]{2,1,0:T(8,128)(2,1)}), bf16[2,24,16384]{2,1,0:T(8,128)(2,1)}) %all-reduce.12.cloned.1.call-update) | async-done | bytes 1572880 | tf_op jit(solution)/shard_map/psum | solution.py:149
  477.4 3.4 select_reduce_fusion.7
  488.9 31.2 %fusion.136 = f32[128,48]{0,1:T(8,128)S(1)} fusion(f32[24,16384]{1,0:T(8,128)S(1)} %fusion.402, f32[24,16384]{1,0:T(8,128)S(1)} %get-tuple-element.88, f32[24,16384]{1,0:T(8,128)S(1)} %get-tuple-element.87, f32[16,8,256,128]{3,2,1,0:T(8,128)} %bitcast.372, f32[128]{0:T(128)S(1)} %dynamic_slice.14), kind=kOutput, calls=%fused_computation.187 | convolution fusion | flops 2420643840 | bytes 21520896 | tf_op jit(solution)/shard_map/sf,kf->sk/dot_general | solution.py:116
  520.1 23.8 %fusion.12 = f32[48,32768]{1,0:T(8,128)S(1)} fusion(f32[128,48]{0,1:T(8,128)S(1)} %fusion.136, f32[16,8,256,128]{3,2,1,0:T(8,128)} %bitcast.373), kind=kOutput, calls=%fused_computation.20 | convolution fusion | flops 2415919104 | bytes 23093248 | tf_op jit(solution)/shard_map/sk,sf->kf/dot_general | solution.py:120
  545.6 43.0 %all-reduce.14.cloned.1.call-done = bf16[2,24,16384]{2,1,0:T(8,128)(2,1)} async-done(((bf16[2,24,16384]{2,1,0:T(8,128)(2,1)}), bf16[2,24,16384]{2,1,0:T(8,128)(2,1)}) %all-reduce.14.cloned.1.call-update) | async-done | bytes 1572880 | tf_op jit(solution)/shard_map/psum | solution.py:149
  588.6 3.4 select_reduce_fusion.6
  600.2 31.5 %fusion.141 = f32[128,48]{0,1:T(8,128)S(1)} fusion(f32[24,16384]{1,0:T(8,128)S(1)} %fusion.403, f32[24,16384]{1,0:T(8,128)S(1)} %get-tuple-element.86, f32[24,16384]{1,0:T(8,128)S(1)} %get-tuple-element.85, f32[16,8,256,128]{3,2,1,0:T(8,128)} %bitcast.374, f32[128]{0:T(128)S(1)} %dynamic_slice.14), kind=kOutput, calls=%fused_computation.188 | convolution fusion | flops 2420643840 | bytes 21520896 | tf_op jit(solution)/shard_map/sf,kf->sk/dot_general | solution.py:116
  631.6 23.8 %fusion.8 = f32[48,32768]{1,0:T(8,128)S(1)} fusion(f32[128,48]{0,1:T(8,128)S(1)} %fusion.141, f32[16,8,256,128]{3,2,1,0:T(8,128)} %bitcast.375), kind=kOutput, calls=%fused_computation.16 | convolution fusion | flops 2415919104 | bytes 23093248 | tf_op jit(solution)/shard_map/sk,sf->kf/dot_general | solution.py:120
  657.9 3.4 collective-permute-start
  664.4 35.7 %all-reduce.16.cloned.1.call-done = bf16[2,24,16384]{2,1,0:T(8,128)(2,1)} async-done(((bf16[2,24,16384]{2,1,0:T(8,128)(2,1)}), bf16[2,24,16384]{2,1,0:T(8,128)(2,1)}) %all-reduce.16.cloned.1.call-update) | async-done | bytes 1572880 | tf_op jit(solution)/shard_map/psum | solution.py:149
  700.1 3.4 select_reduce_fusion.5
  711.6 31.1 %fusion.146 = f32[128,48]{0,1:T(8,128)S(1)} fusion(f32[24,16384]{1,0:T(8,128)S(1)} %fusion.404, f32[24,16384]{1,0:T(8,128)S(1)} %get-tuple-element.84, f32[24,16384]{1,0:T(8,128)S(1)} %get-tuple-element.83, f32[16,8,256,128]{3,2,1,0:T(8,128)} %bitcast.376, f32[128]{0:T(128)S(1)} %dynamic_slice.14), kind=kOutput, calls=%fused_computation.189 | convolution fusion | flops 2420643840 | bytes 21520896 | tf_op jit(solution)/shard_map/sf,kf->sk/dot_general | solution.py:116
  742.7 23.8 %fusion.4 = f32[48,32768]{1,0:T(8,128)S(1)} fusion(f32[128,48]{0,1:T(8,128)S(1)} %fusion.146, f32[16,8,256,128]{3,2,1,0:T(8,128)} %bitcast.377), kind=kOutput, calls=%fused_computation.12 | convolution fusion | flops 2415919104 | bytes 23093248 | tf_op jit(solution)/shard_map/sk,sf->kf/dot_general | solution.py:120
  770.1 41.1 %all-reduce.18.cloned.1.call-done = bf16[2,24,16384]{2,1,0:T(8,128)(2,1)} async-done(((bf16[2,24,16384]{2,1,0:T(8,128)(2,1)}), bf16[2,24,16384]{2,1,0:T(8,128)(2,1)}) %all-reduce.18.cloned.1.call-update) | async-done | bytes 1572880 | tf_op jit(solution)/shard_map/psum | solution.py:149
  827.8 35.8 %fusion.151 = f32[128,48]{0,1:T(8,128)S(1)} fusion(f32[24,16384]{1,0:T(8,128)} %fusion.405, f32[24,16384]{1,0:T(8,128)} %get-tuple-element.82, f32[24,16384]{1,0:T(8,128)} %get-tuple-element.81, f32[16,8,256,128]{3,2,1,0:T(8,128)} %bitcast.378, f32[128]{0:T(128)S(1)} %dynamic_slice.14), kind=kOutput, calls=%fused_computation.190 | convolution fusion | flops 2420643840 | bytes 21520896 | tf_op jit(solution)/shard_map/sf,kf->sk/dot_general | solution.py:116
  863.6 24.0 %fusion = f32[48,32768]{1,0:T(8,128)S(1)} fusion(f32[128,48]{0,1:T(8,128)S(1)} %fusion.151, f32[16,8,256,128]{3,2,1,0:T(8,128)} %bitcast.379), kind=kOutput, calls=%fused_computation.8 | convolution fusion | flops 2415919104 | bytes 23093248 | tf_op jit(solution)/shard_map/sk,sf->kf/dot_general | solution.py:120
  890.0 3.4 gather_fusion
  896.7 38.7 %all-reduce.22.cloned.1.call-done = (bf16[2,128,128]{1,2,0:T(8,128)(2,1)}, bf16[2,128,128]{1,2,0:T(8,128)(2,1)}, bf16[2,24,16384]{2,1,0:T(8,128)(2,1)}) async-done(((bf16[2,128,128]{1,2,0:T(8,128)(2,1)}, bf16[2,128,128]{1,2,0:T(8,128)(2,1)}, bf16[2,24,16384]{2,1,0:T(8,128)(2,1)}), (bf16[2,128,128]{1,2,0:T(8,128)(2,1)}, bf16[2,128,128]{1,2,0:T(8,128)(2,1)}, ...) | async-done | bytes 1703952 | tf_op jit(solution)/shard_map/psum | solution.py:285
  939.4 3.3 convolution_bitcast_fusion.7
  942.8 30.9 %all-gather.1 = bf16[192,24]{1,0:T(8,128)(2,1)S(1)} all-gather(bf16[24,24]{1,0:T(8,128)(2,1)S(1)} %fusion.370), channel_id=3, replica_groups=mesh['src'=4,'tile'=8] {'tile'}, dimensions={0}, use_global_device_ids=true | all-gather | bytes 10368 | tf_op jit(solution)/shard_map/all_gather | solution.py:260
  992.7 4.0 fusion.123
  1002.6 5.1 convolution_bitcast_fusion.5
  1007.7 4.2 fusion.88
  1013.8 5.1 convolution_bitcast_fusion.4
  1018.9 3.8 fusion.96
  1025.1 30.9 %all-reduce.20.cloned.1.call-done = (bf16[2,128,128]{1,2,0:T(8,128)(2,1)}, bf16[2,128,128]{1,2,0:T(8,128)(2,1)}) async-done(((bf16[2,128,128]{1,2,0:T(8,128)(2,1)}, bf16[2,128,128]{1,2,0:T(8,128)(2,1)}), (bf16[2,128,128]{1,2,0:T(8,128)(2,1)}, bf16[2,128,128]{1,2,0:T(8,128)(2,1)})) %all-reduce.20.cloned.1.call-update) | async-done | bytes 131088 | tf_op jit(solution)/shard_map/psum | solution.py:308
  1059.3 3.4 collective-permute-start.2
  1064.6 3.7 collective-permute-done.3
  (591 shorter events, 431.5 us)
Async XLA Ops:
  7.2 32.8 %copy-start = (s32[512,2]{0,1:T(2,128)S(1)}, s32[512,2]{0,1:T(2,128)}, u32[]{:S(2)}) copy-start(s32[512,2]{0,1:T(2,128)} %param.18) | copy-start | bytes 12292
  7.2 470.2 %all-reduce.12.cloned.1.call-start = ((), (), s32[]{:S(2)}) async-start(), calls=%async_computation | async-start | bytes 3145728 | tf_op jit(solution)/shard_map/psum | solution.py:149
  11.9 356.6 %copy-start.19 = (f32[512]{0:T(512)S(1)}, f32[512]{0:T(512)}, u32[]{:S(2)}) copy-start(f32[512]{0:T(512)} %param.19) | copy-start | bytes 6148
  431.7 157.0 %all-reduce.14.cloned.1.call-start = ((), (), s32[]{:S(2)}) async-start(), calls=%async_computation.1 | async-start | bytes 3145728 | tf_op jit(solution)/shard_map/psum | solution.py:149
  477.4 9.7 copy-start.3
  545.6 154.6 %all-reduce.16.cloned.1.call-start = ((), (), s32[]{:S(2)}) async-start(), calls=%async_computation.2 | async-start | bytes 3145728 | tf_op jit(solution)/shard_map/psum | solution.py:149
  588.6 9.7 copy-start.4
  657.1 154.1 %all-reduce.18.cloned.1.call-start = ((), (), s32[]{:S(2)}) async-start(), calls=%async_computation.3 | async-start | bytes 3145728 | tf_op jit(solution)/shard_map/psum | solution.py:149
  657.9 110.9 %collective-permute-start = (bf16[64,64]{1,0:T(8,128)(2,1)S(1)}, bf16[64,64]{1,0:T(8,128)(2,1)S(1)}, u32[]{:S(2)}, u32[]{:S(2)}) collective-permute-start(bf16[64,64]{1,0:T(8,128)(2,1)S(1)} %get-tuple-element.111), channel_id=1, source_target_pairs={{0,1},{1,2},{2,3},{3,4},{4,5},{5,6},{6,7},{8,9},{9,10},{10,11},{11... | collective-permute-start | bytes 24584 | tf_op jit(solution)/shard_map/ppermute | solution.py:32
  661.3 107.5 %collective-permute-start.1 = (bf16[64,64]{1,0:T(8,128)(2,1)S(1)}, bf16[64,64]{1,0:T(8,128)(2,1)S(1)}, u32[]{:S(2)}, u32[]{:S(2)}) collective-permute-start(bf16[64,64]{1,0:T(8,128)(2,1)S(1)} %get-tuple-element.112), channel_id=1, source_target_pairs={{1,0},{2,1},{3,2},{4,3},{5,4},{6,5},{7,6},{9,8},{10,9},{11,10},{12... | collective-permute-start | bytes 24584 | tf_op jit(solution)/shard_map/ppermute | solution.py:34
  663.6 105.4 %copy-start.11 = (bf16[384,128]{1,0:T(8,128)(2,1)}, bf16[384,128]{1,0:T(8,128)(2,1)S(1)}, u32[]{:S(2)}) copy-start(bf16[384,128]{1,0:T(8,128)(2,1)S(1)} %fusion.364) | copy-start | bytes 294916
  700.1 9.7 copy-start.2
  768.1 121.9 %all-gather.7.cloned.1.call-start = ((), (), s32[]{:S(2)}) async-start(), calls=%async_computation.5 | async-start | bytes 3538944 | tf_op jit(solution)/shard_map/all_gather | solution.py:259
  827.7 107.7 %all-reduce.22.cloned.1.call-start = ((), (), s32[]{:S(2)}) async-start(), calls=%async_computation.7 | async-start | bytes 3407872 | tf_op jit(solution)/shard_map/psum | solution.py:285
  889.3 88.9 %all-gather.5.cloned.1.call-start = ((), (), s32[]{:S(2)}) async-start(), calls=%async_computation.4 | async-start | bytes 3932160 | tf_op jit(solution)/shard_map/all_gather | solution.py:160
  889.9 4.8 copy-start.20
  889.9 4.8 copy-start.21
  896.0 160.0 %all-reduce.20.cloned.1.call-start = ((), (), s32[]{:S(2)}) async-start(), calls=%async_computation.6 | async-start | bytes 262144 | tf_op jit(solution)/shard_map/psum | solution.py:308
  980.6 3.8 copy-start.5
  980.6 3.8 copy-start.6
  982.0 0.9 copy-start.10
  984.4 1.2 copy-start.17
  988.9 3.2 copy-start.8
  996.7 3.2 copy-start.7
  999.9 0.8 copy-start.18
  1018.9 4.2 copy-start.16
  1018.9 38.9 %copy-start.12 = (bf16[384,128]{1,0:T(8,128)(2,1)S(1)}, bf16[384,128]{1,0:T(8,128)(2,1)}, u32[]{:S(2)}) copy-start(bf16[384,128]{1,0:T(8,128)(2,1)} %copy-done.11) | copy-start | bytes 294916
  1024.4 39.6 %copy-start.14 = (bf16[64,256]{1,0:T(8,128)(2,1)S(1)}, bf16[64,256]{1,0:T(8,128)(2,1)}, u32[]{:S(2)}) copy-start(bf16[64,256]{1,0:T(8,128)(2,1)} %get-tuple-element.106) | copy-start | bytes 98308
  1024.4 39.6 %copy-start.15 = (bf16[64,256]{1,0:T(8,128)(2,1)S(1)}, bf16[64,256]{1,0:T(8,128)(2,1)}, u32[]{:S(2)}) copy-start(bf16[64,256]{1,0:T(8,128)(2,1)} %get-tuple-element.108) | copy-start | bytes 98308
  1056.9 12.3 %copy-start.1 = (s32[512,2]{0,1:T(2,128)S(1)}, s32[512,2]{0,1:T(2,128)}, u32[]{:S(2)}) copy-start(s32[512,2]{0,1:T(2,128)} %param.18) | copy-start | bytes 12292
  1059.3 5.3 collective-permute-start.2
  1062.6 5.6 collective-permute-start.3
  (3 other events, 2.3 us)
Sparse Core Ops, SparseCore 0:
  431.8 45.5 all-reduce.11
  545.7 42.8 all-reduce.13
  657.2 42.8 all-reduce.15
  768.3 42.8 all-reduce.17
  827.8 60.4 all-gather.6
  891.4 43.9 all-reduce.21
  936.9 28.5 all-gather.4
  1024.5 31.4 all-reduce.19
where the time goes:
time: 1090 us; the launch traced here: 1080 us
  local copies, waits for them, and re-layouts  355 us (33%)
  matrix products  331 us (30%)
  waiting for transfers between devices  239 us (22%)
  other arithmetic  89.1 us (8%)
  blocking collectives  30.9 us (3%)
  between operations  20.9 us (2%)
    gather x384, local copies, waits for them, and re-layouts  328 us
    psum x4, waiting for transfers between devices, synthesize(): lax.psum(spread_terms(windows, products).astype(jnp.bfloat16), 'src')  165 us
    dot_general x5, matrix products, pupil_products(): return jnp.einsum('sf,kf->sk', windows, stacked, precision=EXACT_MODE)  161 us
    dot_general x5, matrix products, spread_terms(): spread = jnp.einsum('sk,sf->kf', products, windows, precision=EXACT_MODE)  120 us
    psum x1, waiting for transfers between devices, on_device(): lax.psum(partial_im.astype(jnp.bfloat16), 'src').astype(jnp.float32)  38.7 us
    all_gather x1, blocking collectives, on_device(): received_mixing = lax.all_gather(mixing[None], 'tile', axis=0, tiled=True)  30.9 us
    psum x1, waiting for transfers between devices, on_device(): lax.psum(jnp.stack(grad_re_list).astype(jnp.bfloat16), 'src')  30.9 us
    mul x1, other arithmetic, pupil_grid(): inside * jnp.cos(phase_angle)  27.4 us
  transfers between devices with their start and end apart: 12, of which 7 were waited for; matrix products, arithmetic and copies ran while one was open for 14% of the time, Pallas kernels for 0%

commit v1 on v0

v1 whole, which is shorter than its diff:
```python
import functools
import math

import jax
import jax.numpy as jnp
import ml_dtypes
import numpy as np
from jax import lax
from jax.experimental import pallas as pl
from jax.experimental.pallas import tpu as pltpu
from jax.sharding import PartitionSpec as P

KB = 128
NR = 24
NZ = 37
RAD = 40
SHIFT = 24
HALO = 64
ITERS = 4
TS = 256
LAGS = 2 * SHIFT + 1
LP = 64
DISC = 88

STEEPNESS = 4.0
THRESHOLD = 0.5
RIDGE_SHARE = 0.001
F32 = jnp.float32
BF16 = jnp.bfloat16


def with_halo(cells, sides, width):
    for axis, dim in sides:
        count = lax.axis_size(axis)
        ends = count - 1
        head = lax.slice_in_dim(cells, 0, width, axis=dim)
        tail = lax.slice_in_dim(cells, cells.shape[dim] - width, cells.shape[dim], axis=dim)
        cells = jnp.concatenate(
            [
                lax.ppermute(tail, axis, [(i, (i + 1) % count) for i in range(ends)]),
                cells,
                lax.ppermute(head, axis, [((i + 1) % count, i) for i in range(ends)]),
            ],
            axis=dim,
        )
    return cells


def noll_terms(term_count):
    listing = []
    degree = 0
    while len(listing) < term_count:
        for azimuth in range(degree % 2, degree + 1, 2):
            if azimuth == 0:
                listing.append((degree, 0, 0))
            else:
                for repeat in range(2):
                    number = len(listing) + 1
                    listing.append((degree, azimuth, 2 if number % 2 == 0 else 1))
        degree += 1
    return listing[:term_count]


def radial_terms(degree, azimuth):
    powers = []
    for counter in range((degree - azimuth) // 2 + 1):
        factor = (
            (-1) ** counter
            * math.factorial(degree - counter)
            / (
                math.factorial(counter)
                * math.factorial((degree + azimuth) // 2 - counter)
                * math.factorial((degree - azimuth) // 2 - counter)
            )
        )
        powers.append((degree - 2 * counter, factor))
    return powers


@functools.lru_cache(None)
def zernike_table():
    u = (np.arange(DISC) - RAD)[:, None]
    v = (np.arange(KB) - RAD)[None, :]
    inside = (u * u + v * v <= RAD * RAD).astype(np.float64)
    rho = np.sqrt(u * u + v * v) / RAD
    theta = np.arctan2(v + 0.0 * u, u + 0.0 * v)
    planes = []
    for degree, azimuth, parity in noll_terms(NZ):
        radial = sum(f * rho**e for e, f in radial_terms(degree, azimuth))
        if azimuth == 0:
            plane = math.sqrt(degree + 1.0) * radial
        else:
            turn = np.cos if parity == 2 else np.sin
            plane = math.sqrt(2.0 * degree + 2.0) * radial * turn(azimuth * theta)
        planes.append(plane * inside)
    planes.append(inside)
    return np.stack(planes).astype(np.float32)


def split_table(table, axis):
    high = table.astype(ml_dtypes.bfloat16)
    low = (table - high.astype(np.float64)).astype(ml_dtypes.bfloat16)
    return np.concatenate([high, high, low], axis=axis)


@functools.lru_cache(None)
def dft_tables():
    f = np.arange(KB)
    angle = 2.0 * np.pi / KB * ((f[:, None] * f[None, :]) % KB)
    c, s = np.cos(angle), np.sin(angle)
    keep = np.arange(LP) < LAGS
    cy, sy = c[:LP] * keep[:, None], s[:LP] * keep[:, None]
    scale = 1.0 / (KB * KB)
    full = np.block([[c, -s], [s, c]])
    lag = np.block([[cy, -sy], [sy, cy]])
    inv_lag = np.block([[cy.T, sy.T], [-sy.T, cy.T]]) * scale
    inv_full = np.block([[c, s], [-s, c]]) * scale
    left_full = np.concatenate([c, s], axis=0)
    left_lag = np.concatenate([cy.T, sy.T], axis=0)
    left_inv = np.concatenate([cy, sy], axis=0)
    return (
        split_table(full, 0),
        split_table(lag, 0),
        split_table(inv_lag, 0),
        split_table(inv_full, 0),
        split_table(left_full, 1),
        split_table(left_lag, 1),
        split_table(left_inv, 1),
    )


def halves(x):
    high = x.astype(BF16)
    return high, (x - high.astype(F32)).astype(BF16)


def right_mul(x, table, passes):
    if passes == 1:
        return jnp.dot(x.astype(BF16), table[: x.shape[1]], preferred_element_type=F32)
    high, low = halves(x)
    return jnp.dot(
        jnp.concatenate([high, low, high], axis=1), table, preferred_element_type=F32
    )


def left_mul(table, x, passes):
    if passes == 1:
        return jnp.dot(table[:, : x.shape[0]], x.astype(BF16), preferred_element_type=F32)
    high, low = halves(x)
    return jnp.dot(
        table, jnp.concatenate([high, low, high], axis=0), preferred_element_type=F32
    )


def nt_mul(x, y):
    xh, xl = halves(x)
    yh, yl = halves(y)
    dims = (((1,), (1,)), ((), ()))
    return (
        lax.dot_general(xh, yh, dims, preferred_element_type=F32)
        + lax.dot_general(xl, yh, dims, preferred_element_type=F32)
        + lax.dot_general(xh, yl, dims, preferred_element_type=F32)
    )


def small_mul(m, x):
    mh, ml = halves(m)
    xh, xl = halves(x)
    return (
        jnp.dot(mh, xh, preferred_element_type=F32)
        + jnp.dot(ml, xh, preferred_element_type=F32)
        + jnp.dot(mh, xl, preferred_element_type=F32)
    )


def forward_turn(t):
    n = t.shape[0] // 2
    return t[:n, :KB] + t[n:, KB:], t[:n, KB:] - t[n:, :KB]


def inverse_turn(t):
    n = t.shape[0] // 2
    return jnp.concatenate([t[:n, :KB] - t[n:, KB:], t[:n, KB:] + t[n:, :KB]], axis=1)


def eliminate(gram, floor):
    row = lax.broadcasted_iota(jnp.int32, (NR, KB), 0)
    lane = lax.broadcasted_iota(jnp.int32, (NR, KB), 1)
    aug = jnp.concatenate([gram, jnp.zeros((NR, KB - NR), F32)], axis=1)
    aug = aug + jnp.where(lane == row + NR, 1.0, 0.0)
    rowid = lax.broadcasted_iota(jnp.int32, (NR, 1), 0)
    scales = jnp.zeros((NR, 1), F32)
    for j in range(NR):
        pivot_row = aug[j : j + 1, :]
        pivot = pivot_row[:, j : j + 1]
        good = pivot > floor
        safe = jnp.where(good, pivot, 1.0)
        inverse = jnp.where(good, 1.0 / safe, 0.0)
        root = jnp.where(good, lax.rsqrt(safe), 0.0)
        factor = jnp.where(rowid > j, aug[:, j : j + 1] * inverse, 0.0)
        aug = aug - factor * pivot_row
        scales = jnp.where(rowid == j, root, scales)
    return aug * scales


def synth_kernel(
    slit_ref, zern_ref, basis_ref, block_ref, points_ref, weight_ref,
    full, lag, inv_lag, inv_full, left_full, left_lag, left_inv,
    out_ref, y_ref, z_ref, s_ref, u_ref, pre_ref, pim_ref, *, gpasses,
):
    lane2 = lax.broadcasted_iota(jnp.int32, (1, KB), 1)
    slit = slit_ref[0]
    waves = zern_ref[slit, 0] * basis_ref[0]
    for z in range(1, NZ):
        waves = waves + zern_ref[slit, z] * basis_ref[z]
    inside = basis_ref[NZ]
    angle = 2.0 * math.pi * waves
    pr = inside * jnp.cos(angle)
    pi = inside * jnp.sin(angle)
    p40 = (pr[80:81, 40:41], pi[80:81, 40:41])
    m40 = (pr[0:1, 40:41], pi[0:1, 40:41])
    q40 = (pr[40:41, 80:81], pi[40:41, 80:81])
    n40 = (pr[40:41, 0:1], pi[40:41, 0:1])
    pupil = jnp.concatenate([pr, pi], axis=1)
    pupil = jnp.concatenate([pupil, jnp.zeros((KB - DISC, 2 * KB), F32)], axis=0)
    hat = forward_turn(left_mul(left_full[...], right_mul(pupil, full[...], 3), 3))
    pre_ref[...] = hat[0]
    pim_ref[...] = hat[1]
    total = jnp.sum(weight_ref[...], axis=1, keepdims=True)
    weight = weight_ref[...] / (math.pi * RAD * RAD * total)
    px = SHIFT - points_ref[0:1, :]
    py = SHIFT - points_ref[1:2, :]
    count = points_ref.shape[1]
    hot_x = lax.broadcasted_iota(jnp.int32, (LP, count), 0) == px
    hot_y = (lax.broadcasted_iota(jnp.int32, (KB, count), 0) % LP) == py
    omega = nt_mul(jnp.where(hot_x, weight, 0.0), jnp.where(hot_y, 1.0, 0.0))
    omega_cat = jnp.concatenate([omega[i : i + 1] for i in range(LAGS)], axis=1)

    def times(scalar, re, im, conj):
        a, b = scalar
        b = -b if conj else b
        return a * re - b * im, a * im + b * re

    def start(k, carry):
        re, im = block_ref[0, k], block_ref[1, k]
        x = jnp.concatenate([re, im], axis=1)
        hr, hi = forward_turn(left_mul(left_full[...], right_mul(x, full[...], 1), 1))
        cr, ci = pre_ref[...], pim_ref[...]
        prod = jnp.concatenate([cr * hr + ci * hi, cr * hi - ci * hr], axis=1)
        c = right_mul(inverse_turn(left_mul(left_inv[...], prod, 1)), inv_lag[...], 1)
        low = lane2 < LAGS
        er = jnp.where(low, pltpu.roll(re[0:1], KB - 40, 1), 0.0)
        ei = jnp.where(low, pltpu.roll(im[0:1], KB - 40, 1), 0.0)
        er, ei = times(p40, er, ei, True)
        edge = er + pltpu.roll(ei, LP, 1)
        rows = lax.broadcasted_iota(jnp.int32, (LP, KB), 0)
        lanes = lax.broadcasted_iota(jnp.int32, (LP, KB), 1)
        c = c - jnp.where(rows == LAGS - 1, edge, 0.0)
        fr, fi = times(q40, re[40 : 40 + LP, 0:1], im[40 : 40 + LP, 0:1], True)
        fall = jnp.where(lanes == LAGS - 1, fr, 0.0) + jnp.where(lanes == LP + LAGS - 1, fi, 0.0)
        z_ref[pl.ds(pl.multiple_of(k * LP, LP), LP), :] = c - jnp.where(rows < LAGS, fall, 0.0)
        return carry

    lax.fori_loop(0, NR, start, 0)

    def load_cat(ref):
        return jnp.concatenate(
            [ref[pl.ds(i, NR, stride=LP), :] for i in range(LAGS)], axis=1
        )

    def store_cat(ref, value):
        for i in range(LAGS):
            ref[pl.ds(i, NR, stride=LP), :] = value[:, i * KB : (i + 1) * KB]

    y_ref[...] = jnp.zeros_like(y_ref)
    power_re, power_im = pre_ref[...], pim_ref[...]
    u_ref[...] = power_re * power_re + power_im * power_im
    ycat = load_cat(z_ref) * omega_cat
    store_cat(y_ref, ycat)

    def apply_gram():
        s_ref[...] = right_mul(y_ref[...], lag[...], gpasses)

        def body(k, carry):
            at = pl.ds(pl.multiple_of(k * LP, LP), LP)
            hr, hi = forward_turn(left_mul(left_lag[...], s_ref[at, :], gpasses))
            power = u_ref[...]
            prod = jnp.concatenate([power * hr, power * hi], axis=1)
            s_ref[at, :] = inverse_turn(left_mul(left_inv[...], prod, gpasses))
            return carry

        lax.fori_loop(0, NR, body, 0, unroll=2)
        z = right_mul(s_ref[...], inv_lag[...], gpasses).reshape(NR, LP, KB)
        y = y_ref[...].reshape(NR, LP, KB)
        lanes = lax.broadcasted_iota(jnp.int32, (1, KB), 1)
        rows = lax.broadcasted_iota(jnp.int32, (1, LP, KB), 1)
        lanes3 = lax.broadcasted_iota(jnp.int32, (1, LP, KB), 2)

        def turned(scalar_a, scalar_b, value):
            cr, ci = times(scalar_a, scalar_b[0], scalar_b[1], True)
            flat = value.reshape(value.shape[0] * value.shape[1], KB)
            swap = pltpu.roll(flat, LP, 1).reshape(value.shape)
            sign = jnp.where(lanes < LP, -1.0, 1.0)
            return cr * value + (ci * sign) * swap

        first, last = y[:, 0:1], y[:, LAGS - 1 : LAGS]
        z = z - jnp.where(rows == 0, turned(m40, p40, last), 0.0)
        z = z - jnp.where(rows == LAGS - 1, last + turned(p40, m40, first), 0.0)
        ar, ai = times(n40, q40[0], q40[1], True)
        lr, li = y[:, :, LAGS - 1 : LAGS], y[:, :, LP + LAGS - 1 : LP + LAGS]
        gr, gi = y[:, :, 0:1], y[:, :, LP : LP + 1]
        z = z - jnp.where(lanes3 == 0, ar * lr - ai * li, 0.0)
        z = z - jnp.where(lanes3 == LP, ar * li + ai * lr, 0.0)
        z = z - jnp.where(lanes3 == LAGS - 1, lr + ar * gr + ai * gi, 0.0)
        z = z - jnp.where(lanes3 == LP + LAGS - 1, li + ar * gi - ai * gr, 0.0)
        z_ref[...] = z.reshape(NR * LP, KB)

    eye = lax.broadcasted_iota(jnp.int32, (NR, NR), 0) == lax.broadcasted_iota(
        jnp.int32, (NR, NR), 1
    )

    def trace_of(m):
        return jnp.sum(
            jnp.sum(jnp.where(eye, m, 0.0), axis=1, keepdims=True), axis=0, keepdims=True
        )

    for it in range(ITERS):
        apply_gram()
        yc, zc = load_cat(y_ref), load_cat(z_ref)
        gram = nt_mul(yc, zc)
        ridge = RIDGE_SHARE * trace_of(gram) / NR + 1e-06
        gram = gram + jnp.where(eye, ridge, 0.0)
        inverse = eliminate(gram, 0.0)[:, NR : 2 * NR]
        projected = small_mul(inverse, zc)
        if it < ITERS - 1:
            store_cat(y_ref, projected * omega_cat)
        else:
            mixing = nt_mul(projected * omega_cat, projected)
            upper = eliminate(mixing, 1e-6 * trace_of(mixing))[:, :NR]
            store_cat(y_ref, small_mul(small_mul(upper, inverse), yc))

    def finish(k, carry):
        y = y_ref[pl.ds(pl.multiple_of(k * LP, LP), LP), :]
        hr, hi = forward_turn(left_mul(left_lag[...], right_mul(y, lag[...], 1), 1))
        cr, ci = pre_ref[...], pim_ref[...]
        prod = jnp.concatenate([cr * hr - ci * hi, cr * hi + ci * hr], axis=1)
        a = right_mul(inverse_turn(left_mul(left_full[...], prod, 1)), inv_full[...], 1)
        last = y[LAGS - 1 : LAGS]
        er = pltpu.roll(jnp.where(lane2 < LP, last, 0.0), 40, 1)
        ei = pltpu.roll(jnp.where(lane2 < LP, 0.0, last), 40 + LP, 1)
        er, ei = times(p40, er, ei, False)
        fr, fi = times(
            q40, y[:, LAGS - 1 : LAGS], y[:, LP + LAGS - 1 : LP + LAGS], False
        )
        rows = lax.broadcasted_iota(jnp.int32, (KB, KB), 0)
        lanes = lax.broadcasted_iota(jnp.int32, (KB, KB), 1)

        def place(column):
            wide = jnp.where(lax.broadcasted_iota(jnp.int32, (LP, KB), 1) == 0, column, 0.0)
            return jnp.concatenate(
                [jnp.zeros((40, KB), F32), wide, jnp.zeros((KB - 40 - LP, KB), F32)], axis=0
            )

        re = a[:, :KB] - jnp.where(rows == 0, er, 0.0) - place(fr)
        im = a[:, KB:] - jnp.where(rows == 0, ei, 0.0) - place(fi)
        out_ref[k] = jnp.concatenate([re, im], axis=1).astype(BF16)
        return carry

    lax.fori_loop(0, NR, finish, 0)


def synthesize(slit, zernike, start_block, source_points, source_weight, gpasses=1):
    tables = [jnp.asarray(t) for t in dft_tables()]
    smem = pl.BlockSpec(memory_space=pltpu.SMEM)
    vmem = pl.BlockSpec(memory_space=pltpu.VMEM)
    return pl.pallas_call(
        functools.partial(synth_kernel, gpasses=gpasses),
        out_shape=jax.ShapeDtypeStruct((NR, KB, 2 * KB), BF16),
        in_specs=[smem, smem] + [vmem] * 11,
        out_specs=vmem,
        scratch_shapes=[
            pltpu.VMEM((NR * LP, KB), F32),
            pltpu.VMEM((NR * LP, KB), F32),
            pltpu.VMEM((NR * LP, 2 * KB), F32),
            pltpu.VMEM((KB, KB), F32),
            pltpu.VMEM((KB, KB), F32),
            pltpu.VMEM((KB, KB), F32),
        ],
        compiler_params=pltpu.CompilerParams(vmem_limit_bytes=50 * 2**20),
        cost_estimate=pl.CostEstimate(
            flops=6 * 10**9, bytes_accessed=8 * 10**6, transcendentals=0
        ),
    )(
        slit, zernike, jnp.asarray(zernike_table()), start_block,
        source_points.T, source_weight[None, :], *tables,
    )


@functools.lru_cache(None)
def phase_tables():
    frequency = np.arange(KB) - KB // 2

    def make(period):
        angle = 2.0 * np.pi / period * np.mod(np.arange(period)[:, None] * frequency, period)
        return [
            turn(angle.astype(np.float32)).astype(ml_dtypes.bfloat16) for turn in (np.cos, np.sin)
        ]

    return make(TS) + make(TS + 2 * HALO)


def row_phases(rank, rows):
    cosine, sine = phase_tables()[:2]
    turn = np.concatenate([cosine, sine], axis=1)
    return lax.dynamic_slice_in_dim(jnp.asarray(turn), rank * rows, rows, 0)


def image_kernel(
    *refs, tiles, rows, scale,
):
    kernel_refs = refs[:tiles]
    (spec_ref, target_ref, turn_ref, back_ref, inverse_ref, adjoint_ref,
     resist_ref, grad_ref, wave_ref, field_ref) = refs[tiles:]

    def parts(block):
        return block[:, :KB].astype(F32), block[:, KB:].astype(F32)

    for t in range(tiles):
        kernels = kernel_refs[t]
        sre = scale * spec_ref[0, t].astype(F32)
        sim = scale * spec_ref[1, t].astype(F32)

        def forward(pair, carry):
            w = []
            for q in range(2):
                kr, ki = parts(kernels[2 * pair + q])
                w.append(((kr * sre + ki * sim).astype(BF16), (kr * sim - ki * sre).astype(BF16)))
            both = jnp.concatenate(
                [jnp.concatenate([w[0][h], w[1][h]], axis=1) for h in range(2)], axis=0
            )
            turned = jnp.dot(turn_ref[...], both, preferred_element_type=F32).astype(BF16)
            for q in range(2):
                at = pl.ds(pl.multiple_of((2 * pair + q) * rows, rows), rows)
                lanes = slice(q * KB, (q + 1) * KB)
                wave_ref[at, :] = jnp.concatenate(
                    [turned[:rows, lanes], turned[rows:, lanes]], axis=1
                )
            return carry

        lax.fori_loop(0, NR // 2, forward, 0, unroll=2)
        field_ref[...] = jnp.dot(wave_ref[...], inverse_ref[...], preferred_element_type=F32)
        intensity = jnp.zeros((rows, TS), F32)
        for k in range(NR):
            field = field_ref[k * rows : (k + 1) * rows, :]
            intensity = intensity + field * field
        resist = 1.0 / (1.0 + jnp.exp(-STEEPNESS * (intensity - THRESHOLD)))
        goal = target_ref[:, t * TS : (t + 1) * TS].astype(F32)
        resist_ref[:, t * TS : (t + 1) * TS] = resist.astype(BF16)
        slope = 4.0 * (resist - goal) * STEEPNESS * resist * (1.0 - resist)
        for k in range(NR):
            at = slice(k * rows, (k + 1) * rows)
            wave_ref[at, :] = (field_ref[at, :] * slope).astype(BF16)
        wave_ref[...] = jnp.dot(
            wave_ref[...], adjoint_ref[...], preferred_element_type=F32
        ).astype(BF16)

        def adjoint(pair, carry):
            acc_re, acc_im = carry
            waves = [
                wave_ref[pl.ds(pl.multiple_of((2 * pair + q) * rows, rows), rows), :]
                for q in range(2)
            ]
            both = jnp.concatenate(
                [
                    jnp.concatenate([waves[q][:, h * KB : (h + 1) * KB] for q in range(2)], axis=1)
                    for h in range(2)
                ],
                axis=0,
            )
            turned = jnp.dot(back_ref[...], both, preferred_element_type=F32)
            for q in range(2):
                kr, ki = parts(kernels[2 * pair + q])
                tr = turned[:KB, q * KB : (q + 1) * KB]
                ti = turned[KB:, q * KB : (q + 1) * KB]
                acc_re = acc_re + kr * tr + ki * ti
                acc_im = acc_im + ki * tr - kr * ti
            return acc_re, acc_im

        zero = jnp.zeros((KB, KB), F32)
        acc_re, acc_im = lax.fori_loop(0, NR // 2, adjoint, (zero, zero))
        grad_ref[t, 0] = acc_re.astype(BF16)
        grad_ref[t, 1] = acc_im.astype(BF16)


def image(kernels, spectra, target, phases, scale):
    tiles = len(kernels)
    rows = target.shape[0]
    c, s = phases[:, :KB], phases[:, KB:]
    turn = jnp.concatenate(
        [jnp.concatenate([c, -s], axis=1), jnp.concatenate([s, c], axis=1)], axis=0
    )
    back = jnp.concatenate(
        [jnp.concatenate([c.T, -s.T], axis=1), jnp.concatenate([s.T, c.T], axis=1)], axis=0
    )
    cosine, sine = [table[HALO : HALO + TS] for table in phase_tables()[2:]]
    inverse = jnp.asarray(np.concatenate([cosine, -sine], axis=1).T.copy())
    adjoint = jnp.asarray(np.concatenate([cosine, sine], axis=1))
    vmem = pl.BlockSpec(memory_space=pltpu.VMEM)
    return pl.pallas_call(
        functools.partial(image_kernel, tiles=tiles, rows=rows, scale=scale),
        out_shape=(
            jax.ShapeDtypeStruct(target.shape, BF16),
            jax.ShapeDtypeStruct((tiles, 2, KB, KB), BF16),
        ),
        in_specs=[vmem] * (tiles + 6),
        out_specs=(vmem, vmem),
        scratch_shapes=[
            pltpu.VMEM((NR * rows, TS), BF16),
            pltpu.VMEM((NR * rows, TS), F32),
        ],
        compiler_params=pltpu.CompilerParams(vmem_limit_bytes=50 * 2**20),
        cost_estimate=pl.CostEstimate(
            flops=2 * 10**9, bytes_accessed=4 * 10**6, transcendentals=0
        ),
    )(*kernels, spectra, target, turn, back, inverse, adjoint)


def patch_gradient(grad_re, grad_im, spectrum_scale, row_table, column_forward):
    back_re = (spectrum_scale * grad_re).astype(jnp.bfloat16)
    back_im = (spectrum_scale * grad_im).astype(jnp.bfloat16)
    back_block = jnp.concatenate(
        [jnp.concatenate([back_re, back_im], axis=1), jnp.concatenate([-back_im, back_re], axis=1)],
        axis=0,
    )
    back_rows = jnp.dot(row_table, back_block, preferred_element_type=jnp.float32).astype(
        jnp.bfloat16
    )
    return jnp.dot(back_rows, column_forward.T, preferred_element_type=jnp.float32)


def tile_kernels(tile_slit, zernike, start_block, source_points, source_weight):
    tiles_here = tile_slit.shape[0]
    group_size = lax.axis_size("src")
    rank = lax.axis_index("src")
    make = lambda slit: synthesize(slit, zernike, start_block, source_points, source_weight)
    if group_size % tiles_here:
        return [make(tile_slit[t : t + 1]) for t in range(tiles_here)]
    place = rank % tiles_here
    own = make(lax.dynamic_slice_in_dim(tile_slit, place, 1, 0))
    held = [own]
    for shift in range(1, tiles_here):
        pairs = [
            (i, i - i % tiles_here + (i + shift) % tiles_here) for i in range(group_size)
        ]
        held.append(lax.ppermute(own, "src", pairs))
    result = []
    for t in range(tiles_here):
        take = held[0]
        for shift in range(1, tiles_here):
            take = jnp.where((place - shift) % tiles_here == t, held[shift], take)
        result.append(take)
    return result


def on_device(mask, target, start_block, zernike, source_points, source_weight, tile_slit):
    group_rank = lax.axis_index("src")
    rows_here = mask.shape[0]
    width_here = mask.shape[1]
    tiles_here = tile_slit.shape[0]
    kernels = tile_kernels(tile_slit, zernike, start_block, source_points, source_weight)
    extended = with_halo(mask, (("tile", 1),), HALO)
    patch_width = TS + 2 * HALO
    spectrum_scale = 1.0 / math.sqrt(TS * patch_width)
    row_table = row_phases(group_rank, rows_here)
    cosine, sine = phase_tables()[2:]
    column_forward = jnp.asarray(np.concatenate([cosine, -sine], axis=1))
    patches = jnp.stack(
        [extended[:, counter * TS : counter * TS + patch_width] for counter in range(tiles_here)]
    )
    columns = jnp.einsum(
        "jxy,yc->jxc", patches, column_forward, preferred_element_type=jnp.float32
    ).astype(jnp.bfloat16)
    row_sums = jnp.einsum("xc,jxd->jcd", row_table, columns, preferred_element_type=jnp.float32)
    partial_re = row_sums[:, :KB, :KB] + row_sums[:, KB:, KB:]
    partial_im = row_sums[:, :KB, KB:] - row_sums[:, KB:, :KB]
    partial = jnp.stack([partial_re, partial_im]).astype(jnp.bfloat16)
    summed = lax.psum(partial, "src")
    resist, grads = image(kernels, summed, target, row_table, spectrum_scale)
    total = lax.psum(grads, "src").astype(jnp.float32)
    accumulated = jnp.zeros((rows_here, width_here + 2 * HALO), jnp.float32)
    for counter in range(tiles_here):
        patch_grad = patch_gradient(
            total[counter, 0], total[counter, 1], spectrum_scale, row_table, column_forward
        )
        accumulated = accumulated.at[:, counter * TS : counter * TS + patch_width].add(patch_grad)
    rim_cols = jnp.concatenate([accumulated[:, :HALO], accumulated[:, width_here + HALO :]], axis=1)
    beside_all = with_halo(rim_cols.astype(jnp.bfloat16), (("tile", 1),), HALO).astype(
        rim_cols.dtype
    )
    from_left = beside_all[:, :HALO]
    from_right = beside_all[:, 3 * HALO :]
    inner_part = accumulated[:, HALO : HALO + width_here]
    inner_part = (
        inner_part
        + jnp.pad(from_left, ((0, 0), (0, width_here - HALO)))
        + jnp.pad(from_right, ((0, 0), (width_here - HALO, 0)))
    )
    return (resist, inner_part.astype(jnp.bfloat16))


def solution(mesh):
    placed = (P("src", "tile"), P("src", "tile"), P(), P(), P(), P(), P("tile"))
    return jax.shard_map(
        on_device,
        mesh=mesh,
        in_specs=placed,
        out_specs=(P("src", "tile"), P("src", "tile")),
        check_vma=False,
    )
```

time: 1090 us -> 228 us (0.21); the launches traced: 1080 us -> 227 us
  local copies, waits for them, and re-layouts: 355 us -> 13.5 us
  matrix products: 331 us -> 1.86 us
  waiting for transfers between devices: 239 us -> 68.9 us
  Pallas kernels: 0 us -> 112 us
  other arithmetic: 89.1 us -> 6.39 us
  blocking collectives: 30.9 us -> 0 us
    gather x386 -> x0, local copies, waits for them, and re-layouts: 332 us -> none
    dot_general x27 -> x2, matrix products: 330 us -> 1.41 us  [patch_gradient(): jnp.dot(back_rows, column_forward.T, preferred_element_type=jnp.float32)]
    psum x6 -> x2, waiting for transfers between devices: 235 us -> 60.8 us  [the longest x1 30.9 us: on_device(): total = lax.psum(grads, 'src').astype(jnp.float32)]
    pallas_call x0 -> x2, Pallas kernels: none -> 112 us  [the longest x1 101 us: synthesize(): pl.pallas_call(functools.partial(synth_kernel, gpasses=gpasses), out_shap...]
    all_gather x1 -> x0, blocking collectives: 30.9 us -> none  [on_device(): received_mixing = lax.all_gather(mixing[None], 'tile', axis=0, tiled=True)]
    mul x5 -> x0, other arithmetic: 30.4 us -> none  [the longest x1 27.4 us: pupil_grid(): inside * jnp.cos(phase_angle)]
    another operation x34 -> x3, other arithmetic: 31.1 us -> 1.33 us  [the longest x2 0.69 us: on_device(): partial = jnp.stack([partial_re, partial_im]).astype(jnp.bfloat16)]
  transfers between devices with their start and end apart: 12 -> 7, of which waited for: 7 -> 5; matrix products, arithmetic and copies ran while one was open for 14% -> 2% of each run, Pallas kernels for 0% -> 0%
where the time goes in v1:
time: 228 us; the launch traced here: 227 us
  Pallas kernels  112 us (49%)
  waiting for transfers between devices  68.9 us (30%)
  between operations  14.3 us (6%)
  local copies, waits for them, and re-layouts  13.5 us (6%)
  starting transfers between devices  10.9 us (5%)
  other arithmetic  6.39 us (3%)
    pallas_call x1, Pallas kernels, synthesize(): pl.pallas_call(functools.partial(synth_kernel, gpasses=gpasses), out_shap...  101 us
    psum x1, waiting for transfers between devices, on_device(): total = lax.psum(grads, 'src').astype(jnp.float32)  30.9 us
    psum x1, waiting for transfers between devices, on_device(): summed = lax.psum(partial, 'src')  29.9 us
    unnamed x40, local copies, waits for them, and re-layouts  11.9 us
    pallas_call x1, Pallas kernels, image(): pl.pallas_call(functools.partial(image_kernel, tiles=tiles, rows=rows, sc...  10.9 us
    ppermute x2, waiting for transfers between devices, with_halo(): lax.ppermute(head, axis, [((i + 1) % count, i) for i in range(ends)])  7.99 us
    ppermute x2, starting transfers between devices, with_halo(): lax.ppermute(tail, axis, [(i, (i + 1) % count) for i in range(ends)])  7.77 us
  transfers between devices with their start and end apart: 7, of which 5 were waited for; matrix products, arithmetic and copies ran while one was open for 2% of the time, Pallas kernels for 0%

profile of v1, /device:TPU:0, one launch (start us, length us, event | category | flops | bytes accessed | tf_op | source)
XLA Modules:
  0.0 227.5 jit_solution(9323858425159142620)
XLA Ops:
  7.2 1.2 dynamic_slice.6.slit_ref
  8.5 0.7 copy-done.3
  9.2 0.7 copy-done.4
  9.8 0.7 copy-done.5
  10.5 1.0 copy-done.6
  11.5 1.0 copy-done.7
  12.5 0.9 copy-done.8
  13.4 0.9 copy-done.9
  14.4 0.9 copy-done.10
  15.3 0.9 copy-done.13
  16.2 0.9 copy-done.14
  17.1 100.6 %shard_map.194 = bf16[24,128,256]{2,1,0:T(8,128)(2,1)S(1)} custom-call(s32[1]{0:T(128)} %dynamic_slice.6.slit_ref, f32[8,37]{1,0:T(8,128)S(1)} %copy-done.3, f32[38,88,128]{2,1,0:T(8,128)} %constant.121.clone.basis_ref, f32[2,24,128,128]{3,2,1,0:T(8,128)} %block_ref.1, s32[2,512]{1,0:T(2,128)S(1)} %bitcast.35, f32[1,512]{1,0:T(1,128)S(1)} %bitcast.36, ...), custom_call_target="tpu_custom_call" | custom-call | flops 6000000000 | bytes 8000000 | tf_op jit(solution)/shard_map/pallas_call | solution.py:376
  117.7 0.5 collective-permute-start
  118.3 4.4 %collective-permute-start.1 = (bf16[64,64]{1,0:T(8,128)(2,1)S(1)}, bf16[64,64]{1,0:T(8,128)(2,1)S(1)}, u32[]{:S(2)}, u32[]{:S(2)}) collective-permute-start(bf16[64,64]{1,0:T(8,128)(2,1)S(1)} %get-tuple-element.51), channel_id=1, source_target_pairs={{0,1},{1,2},{2,3},{3,4},{4,5},{5,6},{6,7},{8,9},{9,10},{10,11},{11... | collective-permute-start | bytes 24584 | tf_op jit(solution)/shard_map/ppermute | solution.py:40
  122.8 1.3 collective-permute-start.2
  124.6 3.8 %collective-permute-done.2 = bf16[64,64]{1,0:T(8,128)(2,1)S(1)} collective-permute-done((bf16[64,64]{1,0:T(8,128)(2,1)S(1)}, bf16[64,64]{1,0:T(8,128)(2,1)S(1)}, u32[]{:S(2)}, u32[]{:S(2)}) %collective-permute-start.2) | collective-permute-done | bytes 8224 | tf_op jit(solution)/shard_map/ppermute | solution.py:42
  128.5 0.4 convolution_bitcast_fusion
  129.0 0.7 pad_maximum_fusion
  129.8 2.8 %broadcast_select_fusion = (bf16[24,128,256]{2,1,0:T(8,128)(2,1)S(1)}, bf16[24,128,256]{2,1,0:T(8,128)(2,1)}) fusion(bf16[24,128,256]{2,1,0:T(8,128)(2,1)} %collective-permute-done, bf16[24,128,256]{2,1,0:T(8,128)(2,1)S(1)} %shard_map.194, pred[]{:T(512)S(6)} %eq.11, pred[]{:T(512)S(6)} %eq.10), kind=kLoop, calls=%fused_computation | loop fusion | flops 1572864 | bytes 6291458 | tf_op jit(solution)/shard_map/jit(_where)/select_n | solution.py:560
  132.5 29.9 %all-reduce.6.cloned.1.call-done.refs_2_ = bf16[2,2,128,128]{3,2,1,0:T(8,128)(2,1)} async-done(((bf16[2,2,128,128]{3,2,1,0:T(8,128)(2,1)}), bf16[2,2,128,128]{3,2,1,0:T(8,128)(2,1)}) %all-reduce.6.cloned.1.call-update) | async-done | bytes 131088 | tf_op jit(solution)/shard_map/psum | solution.py:587
  162.4 1.4 copy-done
  163.8 0.9 copy-done.1
  164.7 0.9 copy-done.12
  165.7 10.9 %shard_map.195 = (bf16[64,512]{1,0:T(8,128)(2,1)}, bf16[2,2,128,128]{3,2,1,0:T(8,128)(2,1)}) custom-call(bf16[24,128,256]{2,1,0:T(8,128)(2,1)S(1)} %copy-done, bf16[24,128,256]{2,1,0:T(8,128)(2,1)S(1)} %get-tuple-element.34.refs_1_, bf16[2,2,128,128]{3,2,1,0:T(8,128)(2,1)S(1)} %copy-done.1, bf16[64,512]{1,0:T(8,128)(2,1)S(1)} %copy-done.2, ...), custom_call_target="tpu_custom_call" | custom-call | flops 2000000000 | bytes 4000000 | tf_op jit(solution)/shard_map/pallas_call | solution.py:509
  176.6 0.6 compare_reduce_fusion
  177.3 30.9 %all-reduce.8.cloned.1.call-done = bf16[2,2,128,128]{3,2,1,0:T(8,128)(2,1)} async-done(((bf16[2,2,128,128]{3,2,1,0:T(8,128)(2,1)}), bf16[2,2,128,128]{3,2,1,0:T(8,128)(2,1)}) %all-reduce.8.cloned.1.call-update) | async-done | bytes 131088 | tf_op jit(solution)/shard_map/psum | solution.py:589
  208.2 0.9 convert_element_type.49
  209.2 1.0 convolution_select_fusion
  210.7 3.4 %collective-permute-start.3 = (bf16[64,64]{1,0:T(8,128)(2,1)S(1)}, bf16[64,64]{1,0:T(8,128)(2,1)S(1)}, u32[]{:S(2)}, u32[]{:S(2)}) collective-permute-start(bf16[64,64]{1,0:T(8,128)(2,1)S(1)} %slice.177), channel_id=1, source_target_pairs={{0,1},{1,2},{2,3},{3,4},{4,5},{5,6},{6,7},{8,9},{9,10},{10,11},{11... | collective-permute-start | bytes 24584 | tf_op jit(solution)/shard_map/ppermute | solution.py:40
  214.1 1.3 collective-permute-start.4
  215.5 4.2 %collective-permute-done.4 = bf16[64,64]{1,0:T(8,128)(2,1)S(1)} collective-permute-done((bf16[64,64]{1,0:T(8,128)(2,1)S(1)}, bf16[64,64]{1,0:T(8,128)(2,1)S(1)}, u32[]{:S(2)}, u32[]{:S(2)}) %collective-permute-start.4) | collective-permute-done | bytes 8224 | tf_op jit(solution)/shard_map/ppermute | solution.py:42
  219.9 0.7 fusion.1
  (50 shorter events, 1.7 us)
Async XLA Ops:
  7.2 155.3 %all-reduce.6.cloned.1.call-start = ((), (), s32[]{:S(2)}) async-start(), calls=%async_computation | async-start | bytes 262144 | tf_op jit(solution)/shard_map/psum | solution.py:587
  8.5 0.7 copy-start.3
  9.2 0.7 copy-start.4
  9.8 0.7 copy-start.5
  10.5 1.0 copy-start.6
  11.5 1.0 copy-start.7
  12.5 0.9 copy-start.8
  13.4 0.9 copy-start.9
  14.4 0.9 copy-start.10
  15.3 0.9 copy-start.13
  16.2 0.9 copy-start.14
  17.1 101.2 %copy-start.18 = (bf16[64,512]{1,0:T(8,128)(2,1)S(1)}, bf16[64,512]{1,0:T(8,128)(2,1)}, u32[]{:S(2)}) copy-start(bf16[64,512]{1,0:T(8,128)(2,1)} %param.23) | copy-start | bytes 196612
  17.1 107.0 %copy-start.15 = (bf16[256,256]{0,1:T(8,128)(2,1)S(1)}, bf16[256,256]{0,1:T(8,128)(2,1)}, u32[]{:S(2)}) copy-start(bf16[256,256]{0,1:T(8,128)(2,1)} %constant.122.clone) | copy-start | bytes 393220
  17.1 111.4 %copy-start.17 = (bf16[384,256,1]{1,0,2:T(8,128)(2,1)S(1)}, bf16[384,256,1]{1,0,2:T(8,128)(2,1)}, u32[]{:S(2)}) copy-start(bf16[384,256,1]{1,0,2:T(8,128)(2,1)} %constant.133) | copy-start | bytes 589828
  117.7 12.0 %collective-permute-start = (bf16[24,128,256]{2,1,0:T(8,128)(2,1)S(1)}, bf16[24,128,256]{2,1,0:T(8,128)(2,1)}, u32[]{:S(2)}, u32[]{:S(2)}) collective-permute-start(bf16[24,128,256]{2,1,0:T(8,128)(2,1)S(1)} %shard_map.194), channel_id=1, source_target_pairs={{0,8},{8,0},{16,24},{24,16},{1,9},{9,1},{17,25},{25,17},{2,10},{10... | collective-permute-start | bytes 4718600 | tf_op jit(solution)/shard_map/ppermute | solution.py:555
  118.3 6.3 %collective-permute-start.1 = (bf16[64,64]{1,0:T(8,128)(2,1)S(1)}, bf16[64,64]{1,0:T(8,128)(2,1)S(1)}, u32[]{:S(2)}, u32[]{:S(2)}) collective-permute-start(bf16[64,64]{1,0:T(8,128)(2,1)S(1)} %get-tuple-element.51), channel_id=1, source_target_pairs={{0,1},{1,2},{2,3},{3,4},{4,5},{5,6},{6,7},{8,9},{9,10},{10,11},{11... | collective-permute-start | bytes 24584 | tf_op jit(solution)/shard_map/ppermute | solution.py:40
  122.8 5.6 %collective-permute-start.2 = (bf16[64,64]{1,0:T(8,128)(2,1)S(1)}, bf16[64,64]{1,0:T(8,128)(2,1)S(1)}, u32[]{:S(2)}, u32[]{:S(2)}) collective-permute-start(bf16[64,64]{1,0:T(8,128)(2,1)S(1)} %get-tuple-element.52), channel_id=1, source_target_pairs={{1,0},{2,1},{3,2},{4,3},{5,4},{6,5},{7,6},{9,8},{10,9},{11,10},{12... | collective-permute-start | bytes 24584 | tf_op jit(solution)/shard_map/ppermute | solution.py:42
  129.7 32.8 %copy-start.2 = (bf16[64,512]{1,0:T(8,128)(2,1)S(1)}, bf16[64,512]{1,0:T(8,128)(2,1)}, u32[]{:S(2)}) copy-start(bf16[64,512]{1,0:T(8,128)(2,1)} %refs_3_.1) | copy-start | bytes 196612
  129.7 32.8 %copy-start.11 = (bf16[256,256]{1,0:T(8,128)(2,1)S(1)}, bf16[256,256]{1,0:T(8,128)(2,1)}, u32[]{:S(2)}) copy-start(bf16[256,256]{1,0:T(8,128)(2,1)} %constant.124.clone.refs_6_) | copy-start | bytes 393220
  129.7 78.5 %all-reduce.8.cloned.1.call-start = ((), (), s32[]{:S(2)}) async-start(), calls=%async_computation.1 | async-start | bytes 262144 | tf_op jit(solution)/shard_map/psum | solution.py:589
  162.4 1.4 copy-start
  163.8 0.9 copy-start.1
  164.7 0.9 copy-start.12
  165.6 43.5 %copy-start.16 = (bf16[256,256]{0,1:T(8,128)(2,1)S(1)}, bf16[256,256]{0,1:T(8,128)(2,1)}, u32[]{:S(2)}) copy-start(bf16[256,256]{0,1:T(8,128)(2,1)} %constant.122.clone) | copy-start | bytes 393220
  165.7 43.5 %copy-start.19 = (bf16[384,256]{1,0:T(8,128)(2,1)S(1)}, bf16[384,256]{1,0:T(8,128)(2,1)}, u32[]{:S(2)}) copy-start(bf16[384,256]{1,0:T(8,128)(2,1)} %constant.123.clone) | copy-start | bytes 589828
  210.7 4.8 %collective-permute-start.3 = (bf16[64,64]{1,0:T(8,128)(2,1)S(1)}, bf16[64,64]{1,0:T(8,128)(2,1)S(1)}, u32[]{:S(2)}, u32[]{:S(2)}) collective-permute-start(bf16[64,64]{1,0:T(8,128)(2,1)S(1)} %slice.177), channel_id=1, source_target_pairs={{0,1},{1,2},{2,3},{3,4},{4,5},{5,6},{6,7},{8,9},{9,10},{10,11},{11... | collective-permute-start | bytes 24584 | tf_op jit(solution)/shard_map/ppermute | solution.py:40
  214.1 5.6 %collective-permute-start.4 = (bf16[64,64]{1,0:T(8,128)(2,1)S(1)}, bf16[64,64]{1,0:T(8,128)(2,1)S(1)}, u32[]{:S(2)}, u32[]{:S(2)}) collective-permute-start(bf16[64,64]{1,0:T(8,128)(2,1)S(1)} %slice.176), channel_id=1, source_target_pairs={{1,0},{2,1},{3,2},{4,3},{5,4},{6,5},{7,6},{9,8},{10,9},{11,10},{12... | collective-permute-start | bytes 24584 | tf_op jit(solution)/shard_map/ppermute | solution.py:42
Sparse Core Ops, SparseCore 0:
  129.8 32.5 all-reduce.5
  176.7 31.3 all-reduce.7

commit v2 on v1

v2 whole, which is shorter than its diff:
```python
import functools
import math

import jax
import jax.numpy as jnp
import ml_dtypes
import numpy as np
from jax import lax
from jax.experimental import pallas as pl
from jax.experimental.pallas import tpu as pltpu
from jax.sharding import PartitionSpec as P

KB = 128
NR = 24
NZ = 37
RAD = 40
SHIFT = 24
HALO = 64
ITERS = 4
TS = 256
LAGS = 2 * SHIFT + 1
LP = 64
DISC = 88

STEEPNESS = 4.0
THRESHOLD = 0.5
RIDGE_SHARE = 0.001
F32 = jnp.float32
BF16 = jnp.bfloat16


def with_halo(cells, sides, width):
    for axis, dim in sides:
        count = lax.axis_size(axis)
        ends = count - 1
        head = lax.slice_in_dim(cells, 0, width, axis=dim)
        tail = lax.slice_in_dim(cells, cells.shape[dim] - width, cells.shape[dim], axis=dim)
        cells = jnp.concatenate(
            [
                lax.ppermute(tail, axis, [(i, (i + 1) % count) for i in range(ends)]),
                cells,
                lax.ppermute(head, axis, [((i + 1) % count, i) for i in range(ends)]),
            ],
            axis=dim,
        )
    return cells


def noll_terms(term_count):
    listing = []
    degree = 0
    while len(listing) < term_count:
        for azimuth in range(degree % 2, degree + 1, 2):
            if azimuth == 0:
                listing.append((degree, 0, 0))
            else:
                for repeat in range(2):
                    number = len(listing) + 1
                    listing.append((degree, azimuth, 2 if number % 2 == 0 else 1))
        degree += 1
    return listing[:term_count]


def radial_terms(degree, azimuth):
    powers = []
    for counter in range((degree - azimuth) // 2 + 1):
        factor = (
            (-1) ** counter
            * math.factorial(degree - counter)
            / (
                math.factorial(counter)
                * math.factorial((degree + azimuth) // 2 - counter)
                * math.factorial((degree - azimuth) // 2 - counter)
            )
        )
        powers.append((degree - 2 * counter, factor))
    return powers


@functools.lru_cache(None)
def zernike_table():
    u = (np.arange(DISC) - RAD)[:, None]
    v = (np.arange(KB) - RAD)[None, :]
    inside = (u * u + v * v <= RAD * RAD).astype(np.float64)
    rho = np.sqrt(u * u + v * v) / RAD
    theta = np.arctan2(v + 0.0 * u, u + 0.0 * v)
    planes = []
    for degree, azimuth, parity in noll_terms(NZ):
        radial = sum(f * rho**e for e, f in radial_terms(degree, azimuth))
        if azimuth == 0:
            plane = math.sqrt(degree + 1.0) * radial
        else:
            turn = np.cos if parity == 2 else np.sin
            plane = math.sqrt(2.0 * degree + 2.0) * radial * turn(azimuth * theta)
        planes.append(plane * inside)
    planes.append(inside)
    return np.stack(planes).astype(np.float32)


@functools.lru_cache(None)
def dft_tables():
    f = np.arange(KB)
    angle = 2.0 * np.pi / KB * ((f[:, None] * f[None, :]) % KB)
    return np.cos(angle).astype(np.float32), np.sin(angle).astype(np.float32)


def halves(x):
    high = x.astype(BF16)
    return high, (x - high.astype(F32)).astype(BF16)


def dot(x, y):
    return jnp.dot(x.astype(BF16), y.astype(BF16), preferred_element_type=F32)


def nt_mul(x, y):
    xh, xl = halves(x)
    yh, yl = halves(y)
    dims = (((1,), (1,)), ((), ()))
    return (
        lax.dot_general(xh, yh, dims, preferred_element_type=F32)
        + lax.dot_general(xl, yh, dims, preferred_element_type=F32)
        + lax.dot_general(xh, yl, dims, preferred_element_type=F32)
    )


def small_mul(m, x):
    mh, ml = halves(m)
    xh, xl = halves(x)
    return (
        jnp.dot(mh, xh, preferred_element_type=F32)
        + jnp.dot(ml, xh, preferred_element_type=F32)
        + jnp.dot(mh, xl, preferred_element_type=F32)
    )


def forward_turn(t):
    n = t.shape[0] // 2
    return t[:n, :KB] + t[n:, KB:], t[:n, KB:] - t[n:, :KB]


def inverse_turn(t):
    n = t.shape[0] // 2
    return jnp.concatenate([t[:n, :KB] - t[n:, KB:], t[:n, KB:] + t[n:, :KB]], axis=1)


def exact_dot(x, y):
    xh, xl = halves(x)
    yh, yl = halves(y)
    return dot(xh, yh) + dot(xl, yh) + dot(xh, yl)


def lane_join(parts):
    return jnp.concatenate(parts, axis=1)


def row_join(parts):
    return jnp.concatenate(parts, axis=0)


def eliminate(gram, floor):
    row = lax.broadcasted_iota(jnp.int32, (NR, KB), 0)
    lane = lax.broadcasted_iota(jnp.int32, (NR, KB), 1)
    aug = lane_join([gram, jnp.zeros((NR, KB - NR), F32)])
    aug = aug + jnp.where(lane == row + NR, 1.0, 0.0)
    scales = jnp.zeros((NR, KB), F32)
    block = 4
    for begin in range(0, NR, block):
        cols = [
            jnp.broadcast_to(aug[:, j : j + 1], (NR, KB)) for j in range(begin, begin + block)
        ]
        for m in range(block):
            j = begin + m
            pivot = cols[m][j : j + 1, :]
            good = pivot > floor
            safe = jnp.where(good, pivot, 1.0)
            inverse = jnp.where(good, 1.0 / safe, 0.0)
            root = jnp.where(good, lax.rsqrt(safe), 0.0)
            factor = jnp.where(row > j, cols[m] * inverse, 0.0)
            aug = aug - factor * aug[j : j + 1, :]
            for later in range(m + 1, block):
                cols[later] = cols[later] - factor * cols[later][j : j + 1, :]
            scales = jnp.where(row == j, root, scales)
    return aug * scales


GROUP = 8


def synth_kernel(
    coef_ref, points_ref, weight_ref, basis_hbm, cos_hbm, sin_hbm, block_hbm,
    out_ref,
    basis_ref, cos_ref, sin_ref, block_ref,
    full, left_full, lag, inv_lag, inv_full, left_lag, left_inv,
    y_ref, z_ref, power_ref, pre_ref, pim_ref, edge_ref, sems,
):
    sources = (basis_hbm, cos_hbm, sin_hbm, block_hbm)
    targets = (basis_ref, cos_ref, sin_ref, block_ref)
    copies = [
        pltpu.make_async_copy(a, b, sems.at[i]) for i, (a, b) in enumerate(zip(sources, targets))
    ]
    for copy in copies:
        copy.start()
    lane = lax.broadcasted_iota(jnp.int32, (1, KB), 1)
    total = jnp.sum(weight_ref[...], axis=1, keepdims=True)
    weight = weight_ref[...] / (math.pi * RAD * RAD * total)
    px = SHIFT - points_ref[0:1, :]
    py = SHIFT - points_ref[1:2, :]
    count = points_ref.shape[1]
    hot_x = lax.broadcasted_iota(jnp.int32, (LP, count), 0) == px
    lag_lane = lax.broadcasted_iota(jnp.int32, (KB, count), 0)
    hot_y = jnp.where(lag_lane < LP, lag_lane, lag_lane - LP) == py
    omega = nt_mul(jnp.where(hot_x, weight, 0.0), jnp.where(hot_y, 1.0, 0.0))
    omega_cat = lane_join([omega[i : i + 1] for i in range(LAGS)])
    copies[0].wait()
    waves = coef_ref[0, 0] * basis_ref[0]
    for z in range(1, NZ):
        waves = waves + coef_ref[0, z] * basis_ref[z]
    inside = basis_ref[NZ]
    angle = 2.0 * math.pi * waves
    pr = inside * jnp.cos(angle)
    pi = inside * jnp.sin(angle)
    p40 = (pr[80:81, 40:41], pi[80:81, 40:41])
    m40 = (pr[0:1, 40:41], pi[0:1, 40:41])
    q40 = (pr[40:41, 80:81], pi[40:41, 80:81])
    n40 = (pr[40:41, 0:1], pi[40:41, 0:1])
    for copy in copies[1:3]:
        copy.wait()
    c, s = cos_ref[...], sin_ref[...]
    scale = 1.0 / (KB * KB)
    full32 = row_join([lane_join([c, -s]), lane_join([s, c])])
    left32 = row_join([c, s])
    full[...] = full32.astype(BF16)
    left_full[...] = left32.astype(BF16)
    inv_full[...] = (scale * row_join([lane_join([c, s]), lane_join([-s, c])])).astype(BF16)
    keep_row = lax.broadcasted_iota(jnp.int32, (LP, KB), 0) < LAGS
    cy, sy = jnp.where(keep_row, c[:LP], 0.0), jnp.where(keep_row, s[:LP], 0.0)
    lag[...] = row_join([lane_join([cy, -sy]), lane_join([sy, cy])]).astype(BF16)
    left_inv[...] = row_join([cy, sy]).astype(BF16)
    keep_lane = lax.broadcasted_iota(jnp.int32, (KB, KB), 1) < LAGS
    ct, st = jnp.where(keep_lane, scale * c, 0.0), jnp.where(keep_lane, scale * s, 0.0)
    inv_lag[...] = row_join(
        [ct + pltpu.roll(st, LP, 1), pltpu.roll(ct, LP, 1) - st]
    ).astype(BF16)
    left_lag[...] = row_join([c[:, :LP], s[:, :LP]]).astype(BF16)
    pupil = row_join([lane_join([pr, pi]), jnp.zeros((KB - DISC, 2 * KB), F32)])
    hat = forward_turn(exact_dot(left32, exact_dot(pupil, full32)))
    pre_ref[...] = hat[0]
    pim_ref[...] = hat[1]
    power_ref[...] = hat[0] * hat[0] + hat[1] * hat[1]

    def times(scalar, re, im, conj):
        a, b = scalar
        b = -b if conj else b
        return a * re - b * im, a * im + b * re

    def entries(shape, items):
        row = lax.broadcasted_iota(jnp.int32, shape, 0)
        col = lax.broadcasted_iota(jnp.int32, shape, 1)
        matrix = jnp.zeros(shape, F32)
        for i, j, value in items:
            matrix = matrix + jnp.where((row == i) & (col == j), value, 0.0)
        return matrix.astype(BF16)

    end = LAGS - 1
    qr, qi = q40
    ar, ai = times(n40, qr, qi, True)
    start_fix = entries(
        (2 * KB, KB),
        [(0, end, -qr), (KB, end, -qi), (0, LP + end, qi), (KB, LP + end, -qr)],
    )
    gram_fix = entries(
        (KB, KB),
        [
            (end, 0, -ar), (LP + end, 0, ai), (LP + end, LP, -ar), (end, LP, -ai),
            (end, end, -1.0), (0, end, -ar), (LP, end, -ai),
            (LP + end, LP + end, -1.0), (LP, LP + end, -ar), (0, LP + end, ai),
        ],
    )
    final_fix = entries(
        (KB, 2 * KB),
        [(end, 0, -qr), (LP + end, 0, qi), (end, KB, -qi), (LP + end, KB, -qr)],
    )

    copies[3].wait()
    left = left_full[...]
    right = full[...]

    def lanes_of(x, g, width):
        return x[:, g * width : (g + 1) * width]

    def start(group, carry):
        base = group * GROUP
        xs = [
            lane_join([block_ref[0, base + g].astype(BF16), block_ref[1, base + g].astype(BF16)])
            for g in range(GROUP)
        ]
        one = dot(row_join(xs), right).astype(BF16)
        two = dot(left, lane_join([one[g * KB : (g + 1) * KB] for g in range(GROUP)]))
        cr, ci = pre_ref[...], pim_ref[...]
        prods = []
        for g in range(GROUP):
            hr, hi = forward_turn(lanes_of(two, g, 2 * KB))
            prods += [(cr * hr + ci * hi).astype(BF16), (cr * hi - ci * hr).astype(BF16)]
        three = dot(left_inv[...], lane_join(prods))
        four = row_join(
            [
                lane_join([inverse_turn(lanes_of(three, g, 2 * KB)).astype(BF16), xs_rows])
                for g, xs_rows in enumerate([x.astype(F32)[40 : 40 + LP].astype(BF16) for x in xs])
            ]
        )
        c = dot(four, row_join([inv_lag[...], start_fix]))
        z_ref[pl.ds(pl.multiple_of(base * LP, GROUP * LP), GROUP * LP), :] = c
        return carry

    lax.fori_loop(0, NR // GROUP, start, 0)
    at_first = pl.ds(0, NR, stride=LP)
    at_last = pl.ds(end, NR, stride=LP)
    within = lane < LAGS
    er = row_join([block_ref[0, k, 0:1, :] for k in range(NR)])
    ei = row_join([block_ref[1, k, 0:1, :] for k in range(NR)])
    er = jnp.where(within, pltpu.roll(er, KB - 40, 1), 0.0)
    ei = jnp.where(within, pltpu.roll(ei, KB - 40, 1), 0.0)
    er, ei = times(p40, er, ei, True)
    z_ref[at_last, :] = z_ref[at_last, :] - (er + pltpu.roll(ei, LP, 1))

    def load_cat(ref):
        return lane_join([ref[pl.ds(i, NR, stride=LP), :] for i in range(LAGS)])

    def store_cat(ref, value):
        for i in range(LAGS):
            ref[pl.ds(i, NR, stride=LP), :] = value[:, i * KB : (i + 1) * KB]

    y_ref[...] = jnp.zeros_like(y_ref)
    store_cat(y_ref, load_cat(z_ref) * omega_cat)

    def turned(scalar_a, scalar_b, value):
        cr, ci = times(scalar_a, scalar_b[0], scalar_b[1], True)
        return cr * value + jnp.where(lane < LP, -ci, ci) * pltpu.roll(value, LP, 1)

    def apply_gram():
        def body(group, carry):
            base = pl.multiple_of(group * GROUP * LP, GROUP * LP)
            at = pl.ds(base, GROUP * LP)
            y = y_ref[at, :].astype(BF16)
            one = dot(y, lag[...]).astype(BF16)
            two = dot(
                left_lag[...], lane_join([one[g * LP : (g + 1) * LP] for g in range(GROUP)])
            )
            power = power_ref[...]
            prods = []
            for g in range(GROUP):
                hr, hi = forward_turn(lanes_of(two, g, 2 * KB))
                prods += [(power * hr).astype(BF16), (power * hi).astype(BF16)]
            three = dot(left_inv[...], lane_join(prods))
            four = row_join(
                [inverse_turn(lanes_of(three, g, 2 * KB)).astype(BF16) for g in range(GROUP)]
            )
            z_ref[at, :] = dot(lane_join([four, y]), row_join([inv_lag[...], gram_fix]))
            return carry

        lax.fori_loop(0, NR // GROUP, body, 0)
        y_first, y_last = y_ref[at_first, :], y_ref[at_last, :]
        z_ref[at_first, :] = z_ref[at_first, :] - turned(m40, p40, y_last)
        z_ref[at_last, :] = z_ref[at_last, :] - (y_last + turned(p40, m40, y_first))

    eye = lax.broadcasted_iota(jnp.int32, (NR, NR), 0) == lax.broadcasted_iota(
        jnp.int32, (NR, NR), 1
    )

    def trace_of(m):
        return jnp.sum(
            jnp.sum(jnp.where(eye, m, 0.0), axis=1, keepdims=True), axis=0, keepdims=True
        )

    for it in range(ITERS):
        apply_gram()
        yc, zc = load_cat(y_ref), load_cat(z_ref)
        gram = nt_mul(yc, zc)
        ridge = RIDGE_SHARE * trace_of(gram) / NR + 1e-06
        gram = gram + jnp.where(eye, ridge, 0.0)
        inverse = eliminate(gram, 0.0)[:, NR : 2 * NR]
        projected = small_mul(inverse, zc)
        if it < ITERS - 1:
            store_cat(y_ref, projected * omega_cat)
        else:
            mixing = nt_mul(projected * omega_cat, projected)
            upper = eliminate(mixing, 1e-6 * trace_of(mixing))[:, :NR]
            store_cat(y_ref, small_mul(small_mul(upper, inverse), yc))

    last = y_ref[at_last, :]
    er = pltpu.roll(jnp.where(lane < LP, last, 0.0), 40, 1)
    ei = pltpu.roll(jnp.where(lane < LP, 0.0, last), 40 + LP, 1)
    er, ei = times(p40, er, ei, False)
    edge_ref[...] = lane_join([er, ei])

    def finish(group, carry):
        base = group * GROUP
        y = y_ref[pl.ds(pl.multiple_of(base * LP, GROUP * LP), GROUP * LP), :].astype(BF16)
        one = dot(y, lag[...]).astype(BF16)
        two = dot(left_lag[...], lane_join([one[g * LP : (g + 1) * LP] for g in range(GROUP)]))
        cr, ci = pre_ref[...], pim_ref[...]
        prods = []
        for g in range(GROUP):
            hr, hi = forward_turn(lanes_of(two, g, 2 * KB))
            prods += [(cr * hr - ci * hi).astype(BF16), (cr * hi + ci * hr).astype(BF16)]
        three = dot(left, lane_join(prods))
        four = row_join(
            [inverse_turn(lanes_of(three, g, 2 * KB)).astype(BF16) for g in range(GROUP)]
        )
        a = dot(four, inv_full[...])
        fix = dot(y, final_fix)
        edges = edge_ref[pl.ds(pl.multiple_of(base, GROUP), GROUP), :]
        for g in range(GROUP):
            top = g * KB
            head = a[top : top + 8]
            first_row = lax.broadcasted_iota(jnp.int32, head.shape, 0) == 0
            head = head - jnp.where(first_row, edges[g : g + 1], 0.0)
            out_ref[base + g] = row_join(
                [
                    head,
                    a[top + 8 : top + 40],
                    a[top + 40 : top + 40 + LP] + fix[g * LP : (g + 1) * LP],
                    a[top + 40 + LP : top + KB],
                ]
            ).astype(BF16)
        return carry

    lax.fori_loop(0, NR // GROUP, finish, 0)


def synthesize(slit, zernike, start_block, source_points, source_weight):
    basis = jnp.asarray(zernike_table())
    cosine, sine = [jnp.asarray(t) for t in dft_tables()]
    smem = pl.BlockSpec(memory_space=pltpu.SMEM)
    vmem = pl.BlockSpec(memory_space=pltpu.VMEM)
    hbm = pl.BlockSpec(memory_space=pl.ANY)
    held = [basis, cosine, sine, start_block]
    tables = [(2 * KB, 2 * KB), (2 * KB, KB), (KB, 2 * KB), (2 * KB, KB),
              (2 * KB, 2 * KB), (2 * KB, LP), (KB, KB)]
    return pl.pallas_call(
        synth_kernel,
        out_shape=jax.ShapeDtypeStruct((NR, KB, 2 * KB), BF16),
        in_specs=[smem, vmem, vmem] + [hbm] * len(held),
        out_specs=vmem,
        scratch_shapes=[pltpu.VMEM(x.shape, x.dtype) for x in held]
        + [pltpu.VMEM(shape, BF16) for shape in tables]
        + [
            pltpu.VMEM((NR * LP, KB), F32),
            pltpu.VMEM((NR * LP, KB), F32),
            pltpu.VMEM((KB, KB), F32),
            pltpu.VMEM((KB, KB), F32),
            pltpu.VMEM((KB, KB), F32),
            pltpu.VMEM((NR, 2 * KB), F32),
            pltpu.SemaphoreType.DMA((len(held),)),
        ],
        compiler_params=pltpu.CompilerParams(vmem_limit_bytes=56 * 2**20),
        cost_estimate=pl.CostEstimate(
            flops=60 * 10**9, bytes_accessed=8 * 10**6, transcendentals=0
        ),
    )(
        lax.dynamic_slice_in_dim(zernike, slit[0], 1, 0),
        source_points.T, source_weight[None, :], *held,
    )


@functools.lru_cache(None)
def phase_tables():
    frequency = np.arange(KB) - KB // 2

    def make(period):
        angle = 2.0 * np.pi / period * np.mod(np.arange(period)[:, None] * frequency, period)
        return [
            turn(angle.astype(np.float32)).astype(ml_dtypes.bfloat16) for turn in (np.cos, np.sin)
        ]

    return make(TS) + make(TS + 2 * HALO)


@functools.lru_cache(None)
def imaging_tables(group):
    cosine, sine, column_cos, column_sin = [t.astype(np.float32) for t in phase_tables()]
    rows = TS // group
    turns, backs = [], []
    for rank in range(group):
        c, s = [t[rank * rows : (rank + 1) * rows] for t in (cosine, sine)]
        turns.append(np.block([[c, -s], [s, c]]))
        backs.append(np.block([[c.T, -s.T], [s.T, c.T]]))
    inner = slice(HALO, HALO + TS)
    inverse = np.concatenate([column_cos[inner], -column_sin[inner]], axis=1).T
    adjoint = np.concatenate([column_cos[inner], column_sin[inner]], axis=1)
    spread = np.concatenate([column_cos, -column_sin], axis=1).T
    return tuple(
        np.ascontiguousarray(t) for t in (np.stack(turns), np.stack(backs), inverse, adjoint, spread)
    )


def image_kernel(
    own_hbm, spec_ref, target_ref, turn_hbm, back_hbm, inverse_hbm, adjoint_hbm, spread_hbm,
    resist_ref, grad_ref,
    held, turn32, back32, inverse32, adjoint32, spread32,
    wave_ref, field_ref, part_ref, got_ref, acc_ref, rim_ref, left_ref, right_ref,
    local_sems, k_send, k_recv, g_send, g_recv, r_send, r_recv,
    *, group, line, tiles, rows, scale,
):
    rank, me = lax.axis_index("src"), lax.axis_index("tile")
    place = lax.rem(rank, tiles)
    right = lax.rem(me + 1, line)
    left = lax.rem(me + line - 1, line)
    loads = [
        (own_hbm, held.at[0]), (turn_hbm.at[rank], turn32), (back_hbm.at[rank], back32),
        (inverse_hbm, inverse32), (adjoint_hbm, adjoint32), (spread_hbm, spread32),
    ]
    loads = [pltpu.make_async_copy(a, b, local_sems.at[i]) for i, (a, b) in enumerate(loads)]
    for load in loads:
        load.start()

    peers = [lax.rem(rank + step, group) for step in range(1, group)]
    barrier = pltpu.get_barrier_semaphore()
    for peer in peers:
        pl.semaphore_signal(
            barrier, inc=1, device_id=(peer, me), device_id_type=pl.DeviceIdType.MESH
        )
    for side in (left, right):
        pl.semaphore_signal(
            barrier, inc=1, device_id=(rank, side), device_id_type=pl.DeviceIdType.MESH
        )
    pl.semaphore_wait(barrier, group - 1 + 2)

    def send(src, dst, send_sem, recv_sem, device):
        copy = pltpu.make_async_remote_copy(
            src_ref=src, dst_ref=dst, send_sem=send_sem, recv_sem=recv_sem,
            device_id=device, device_id_type=pl.DeviceIdType.MESH,
        )
        copy.start()
        return copy

    kernel_copies = [
        send(
            own_hbm, held.at[step], k_send.at[step - 1], k_recv.at[step - 1],
            (rank - place + lax.rem(place + step, tiles), me),
        )
        for step in range(1, tiles)
    ]
    for load in loads:
        load.wait()
    turn = turn32[...].astype(BF16)
    back = back32[...].astype(BF16)
    inverse = inverse32[...].astype(BF16)
    adjoint = adjoint32[...].astype(BF16)

    def parts(block):
        return block[:, :KB].astype(F32), block[:, KB:].astype(F32)

    grad_copies = []
    for slot in range(tiles):
        t = lax.rem(place + tiles - slot, tiles)
        start = pl.multiple_of(t * TS, TS)
        if slot > 0:
            kernel_copies[slot - 1].wait_recv()
        sre = scale * spec_ref[0, t].astype(F32)
        sim = scale * spec_ref[1, t].astype(F32)

        def forward(pair, carry):
            w = []
            for q in range(2):
                kr, ki = parts(held[slot, 2 * pair + q])
                w.append(((kr * sre + ki * sim).astype(BF16), (kr * sim - ki * sre).astype(BF16)))
            both = row_join([lane_join([w[0][h], w[1][h]]) for h in range(2)])
            turned = dot(turn, both).astype(BF16)
            for q in range(2):
                at = pl.ds(pl.multiple_of((2 * pair + q) * rows, rows), rows)
                lanes = slice(q * KB, (q + 1) * KB)
                wave_ref[at, :] = lane_join([turned[:rows, lanes], turned[rows:, lanes]])
            return carry

        lax.fori_loop(0, NR // 2, forward, 0, unroll=2)
        field_ref[...] = dot(wave_ref[...], inverse)

        def energy(k, total):
            field = field_ref[pl.ds(pl.multiple_of(k * rows, rows), rows), :]
            return total + field * field

        intensity = lax.fori_loop(0, NR, energy, jnp.zeros((rows, TS), F32), unroll=4)
        resist = 1.0 / (1.0 + jnp.exp(-STEEPNESS * (intensity - THRESHOLD)))
        goal = target_ref[:, pl.ds(start, TS)].astype(F32)
        resist_ref[:, pl.ds(start, TS)] = resist.astype(BF16)
        slope = 4.0 * (resist - goal) * STEEPNESS * resist * (1.0 - resist)

        def weigh(k, carry):
            at = pl.ds(pl.multiple_of(k * rows, rows), rows)
            wave_ref[at, :] = (field_ref[at, :] * slope).astype(BF16)
            return carry

        lax.fori_loop(0, NR, weigh, 0, unroll=4)
        wave_ref[...] = dot(wave_ref[...], adjoint).astype(BF16)

        def gather(pair, carry):
            acc_re, acc_im = carry
            waves = [
                wave_ref[pl.ds(pl.multiple_of((2 * pair + q) * rows, rows), rows), :]
                for q in range(2)
            ]
            both = row_join(
                [lane_join([waves[q][:, h * KB : (h + 1) * KB] for q in range(2)]) for h in range(2)]
            )
            turned = dot(back, both)
            for q in range(2):
                kr, ki = parts(held[slot, 2 * pair + q])
                tr = turned[:KB, q * KB : (q + 1) * KB]
                ti = turned[KB:, q * KB : (q + 1) * KB]
                acc_re = acc_re + kr * tr + ki * ti
                acc_im = acc_im + ki * tr - kr * ti
            return acc_re, acc_im

        zero = jnp.zeros((KB, KB), F32)
        acc_re, acc_im = lax.fori_loop(0, NR // 2, gather, (zero, zero), unroll=2)
        part_ref[slot, 0] = acc_re.astype(BF16)
        part_ref[slot, 1] = acc_im.astype(BF16)
        grad_copies.append(
            [
                send(
                    part_ref.at[slot], got_ref.at[slot, step], g_send.at[slot, step],
                    g_recv.at[slot, step], (peer, me),
                )
                for step, peer in enumerate(peers)
            ]
        )

    acc_ref[...] = jnp.zeros_like(acc_ref)
    spread = spread32[...].astype(BF16)
    for copies in grad_copies:
        for copy in copies:
            copy.wait_recv()
    for slot in range(tiles):
        t = lax.rem(place + tiles - slot, tiles)
        at = pl.ds(pl.multiple_of(t * TS, TS), TS + 2 * HALO)
        total = part_ref[slot].astype(F32)
        for step in range(1, group):
            total = total + got_ref[(slot - step) % tiles, step - 1].astype(F32)
        total = (scale * total).astype(BF16)
        rows_back = dot(turn, row_join([total[0], total[1]])).astype(BF16)
        patch = dot(lane_join([rows_back[:rows], rows_back[rows:]]), spread)
        acc_ref[:, at] = acc_ref[:, at] + patch

    width = tiles * TS
    lane = lax.broadcasted_iota(jnp.int32, (rows, 2 * HALO), 1)
    low = lane < HALO
    rim_ref[...] = jnp.where(
        low, acc_ref[:, : 2 * HALO], acc_ref[:, width : width + 2 * HALO]
    ).astype(BF16)
    rims = [
        send(rim_ref, left_ref, r_send.at[0], r_recv.at[0], (rank, right)),
        send(rim_ref, right_ref, r_send.at[1], r_recv.at[1], (rank, left)),
    ]
    inner = pltpu.roll(acc_ref[...], width + HALO, 1)[:, :width]
    rims[0].wait_recv()
    rims[1].wait_recv()
    from_left = pltpu.roll(left_ref[...].astype(F32), HALO, 1)
    from_right = pltpu.roll(right_ref[...].astype(F32), HALO, 1)
    from_left = jnp.where(low & (me > 0), from_left, 0.0)
    from_right = jnp.where((lane >= HALO) & (me < line - 1), from_right, 0.0)
    blocks = [
        inner[:, : 2 * HALO] + from_left,
        inner[:, 2 * HALO : width - 2 * HALO],
        inner[:, width - 2 * HALO :] + from_right,
    ]
    grad_ref[...] = lane_join(blocks).astype(BF16)
    for copy in kernel_copies + [c for copies in grad_copies for c in copies] + rims:
        copy.wait_send()


def image(own, spectra, target, scale):
    tiles = spectra.shape[1]
    rows = target.shape[0]
    group, line = lax.axis_size("src"), lax.axis_size("tile")
    tables = [jnp.asarray(t) for t in imaging_tables(group)]
    vmem = pl.BlockSpec(memory_space=pltpu.VMEM)
    hbm = pl.BlockSpec(memory_space=pl.ANY)
    dma = pltpu.SemaphoreType.DMA
    return pl.pallas_call(
        functools.partial(
            image_kernel, group=group, line=line, tiles=tiles, rows=rows, scale=scale
        ),
        out_shape=(
            jax.ShapeDtypeStruct(target.shape, BF16),
            jax.ShapeDtypeStruct(target.shape, BF16),
        ),
        in_specs=[hbm, vmem, vmem] + [hbm] * len(tables),
        out_specs=(vmem, vmem),
        scratch_shapes=[
            pltpu.VMEM((tiles,) + own.shape, BF16),
            pltpu.VMEM(tables[0].shape[1:], F32),
            pltpu.VMEM(tables[1].shape[1:], F32),
            pltpu.VMEM(tables[2].shape, F32),
            pltpu.VMEM(tables[3].shape, F32),
            pltpu.VMEM(tables[4].shape, F32),
            pltpu.VMEM((NR * rows, TS), BF16),
            pltpu.VMEM((NR * rows, TS), F32),
            pltpu.VMEM((tiles, 2, KB, KB), BF16),
            pltpu.VMEM((tiles, group - 1, 2, KB, KB), BF16),
            pltpu.VMEM((rows, tiles * TS + 2 * HALO), F32),
            pltpu.VMEM((rows, 2 * HALO), BF16),
            pltpu.VMEM((rows, 2 * HALO), BF16),
            pltpu.VMEM((rows, 2 * HALO), BF16),
            dma((6,)),
            dma((tiles,)),
            dma((tiles,)),
            dma((tiles, group - 1)),
            dma((tiles, group - 1)),
            dma((2,)),
            dma((2,)),
        ],
        compiler_params=pltpu.CompilerParams(
            vmem_limit_bytes=56 * 2**20, collective_id=0, has_side_effects=True
        ),
        cost_estimate=pl.CostEstimate(
            flops=2 * 10**9, bytes_accessed=4 * 10**6, transcendentals=0
        ),
    )(own, spectra, target, *tables)


def on_device(mask, target, start_block, zernike, source_points, source_weight, tile_slit):
    rank = lax.axis_index("src")
    rows_here = mask.shape[0]
    tiles_here = tile_slit.shape[0]
    patch_width = TS + 2 * HALO
    spectrum_scale = 1.0 / math.sqrt(TS * patch_width)
    extended = with_halo(mask, (("tile", 1),), HALO)
    cosine, sine, column_cos, column_sin = phase_tables()
    row_table = lax.dynamic_slice_in_dim(
        jnp.asarray(np.concatenate([cosine, sine], axis=1)), rank * rows_here, rows_here, 0
    )
    column_forward = jnp.asarray(np.concatenate([column_cos, -column_sin], axis=1))
    patches = jnp.stack(
        [extended[:, counter * TS : counter * TS + patch_width] for counter in range(tiles_here)]
    )
    columns = jnp.einsum(
        "jxy,yc->jxc", patches, column_forward, preferred_element_type=jnp.float32
    ).astype(jnp.bfloat16)
    row_sums = jnp.einsum("xc,jxd->jcd", row_table, columns, preferred_element_type=jnp.float32)
    partial_re = row_sums[:, :KB, :KB] + row_sums[:, KB:, KB:]
    partial_im = row_sums[:, :KB, KB:] - row_sums[:, KB:, :KB]
    partial = jnp.stack([partial_re, partial_im]).astype(jnp.bfloat16)
    slit = lax.dynamic_slice_in_dim(tile_slit, rank % tiles_here, 1, 0)
    partial, slit = lax.optimization_barrier((partial, slit))
    spectra = lax.psum(partial, "src")
    own = synthesize(slit, zernike, start_block, source_points, source_weight)
    return image(own, spectra, target, spectrum_scale)


def solution(mesh):
    placed = (P("src", "tile"), P("src", "tile"), P(), P(), P(), P(), P("tile"))
    return jax.shard_map(
        on_device,
        mesh=mesh,
        in_specs=placed,
        out_specs=(P("src", "tile"), P("src", "tile")),
        check_vma=False,
    )
```

time: 228 us -> 93.7 us (0.41)
  waiting for transfers between devices: 68.9 us -> 3.11 us
  Pallas kernels: 112 us -> 59.4 us
  local copies, waits for them, and re-layouts: 13.5 us -> 5.53 us
  starting transfers between devices: 10.9 us -> 6.16 us
  other arithmetic: 6.39 us -> 1.66 us
    psum x2 -> x1, waiting for transfers between devices: 60.8 us -> 0.02 us  [on_device(): spectra = lax.psum(partial, 'src')]
    pallas_call x2, Pallas kernels: 112 us -> 59.4 us  [the longest x1 37.6 us: synthesize(): pl.pallas_call(synth_kernel, out_shape=jax.ShapeDtypeStruct((NR, KB, 2 *...]
    unnamed x40 -> x4, local copies, waits for them, and re-layouts: 11.9 us -> 2.96 us
    ppermute x2 -> x1, waiting for transfers between devices: 7.99 us -> 3.07 us  [with_halo(): lax.ppermute(head, axis, [((i + 1) % count, i) for i in range(ends)])]
    ppermute x2 -> x1, starting transfers between devices: 7.77 us -> 4.83 us  [with_halo(): lax.ppermute(tail, axis, [(i, (i + 1) % count) for i in range(ends)])]
    select_n x1 -> x0, other arithmetic: 2.79 us -> none  [tile_kernels(): take = jnp.where((place - shift) % tiles_here == t, held[shift], take)]
  transfers between devices with their start and end apart: 7 -> 3, of which waited for: 5 -> 1; matrix products, arithmetic and copies ran while one was open for 2% -> 2% of each run, Pallas kernels for 0% -> 40%
where the time goes in v2:
time: 93.7 us; the launch traced here: 93.3 us
  Pallas kernels  59.4 us (63%)
  between operations  16.1 us (17%)
  starting transfers between devices  6.16 us (7%)
  local copies, waits for them, and re-layouts  5.53 us (6%)
  waiting for transfers between devices  3.11 us (3%)
  other arithmetic  1.66 us (2%)
  matrix products  1.39 us (1%)
    pallas_call x1, Pallas kernels, synthesize(): pl.pallas_call(synth_kernel, out_shape=jax.ShapeDtypeStruct((NR, KB, 2 *...  37.6 us
    pallas_call x1, Pallas kernels, image(): pl.pallas_call(functools.partial(image_kernel, group=group, line=line, ti...  21.8 us
    ppermute x1, starting transfers between devices, with_halo(): lax.ppermute(tail, axis, [(i, (i + 1) % count) for i in range(ends)])  4.83 us
    ppermute x1, waiting for transfers between devices, with_halo(): lax.ppermute(head, axis, [((i + 1) % count, i) for i in range(ends)])  3.07 us
    unnamed x4, local copies, waits for them, and re-layouts  2.96 us
  transfers between devices with their start and end apart: 3, of which 1 were waited for; matrix products, arithmetic and copies ran while one was open for 2% of the time, Pallas kernels for 40%

profile of v2, /device:TPU:0, one launch (start us, length us, event | category | flops | bytes accessed | tf_op | source)
XLA Modules:
  0.0 93.3 jit_solution(13648547069477628990)
XLA Ops:
  7.2 0.0 copy-start
  7.2 0.0 all-reduce.2.cloned.1.call-start
  7.2 0.8 fusion.17
  8.0 4.8 %collective-permute-start = (bf16[64,64]{1,0:T(8,128)(2,1)S(1)}, bf16[64,64]{1,0:T(8,128)(2,1)S(1)}, u32[]{:S(2)}, u32[]{:S(2)}) collective-permute-start(bf16[64,64]{1,0:T(8,128)(2,1)S(1)} %get-tuple-element.10), channel_id=1, source_target_pairs={{0,1},{1,2},{2,3},{3,4},{4,5},{5,6},{6,7},{8,9},{9,10},{10,11},{11... | collective-permute-start | bytes 24584 | tf_op jit(solution)/shard_map/ppermute | solution.py:40
  12.9 1.3 %collective-permute-start.1 = (bf16[64,64]{1,0:T(8,128)(2,1)S(1)}, bf16[64,64]{1,0:T(8,128)(2,1)S(1)}, u32[]{:S(2)}, u32[]{:S(2)}) collective-permute-start(bf16[64,64]{1,0:T(8,128)(2,1)S(1)} %get-tuple-element.11), channel_id=1, source_target_pairs={{1,0},{2,1},{3,2},{4,3},{5,4},{6,5},{7,6},{9,8},{10,9},{11,10},{12... | collective-permute-start | bytes 24584 | tf_op jit(solution)/shard_map/ppermute | solution.py:42
  14.2 1.2 %dynamic_slice.10 = s32[1]{0:T(128)} dynamic-slice(s32[2]{0:T(128)} %param.23, s32[]{:T(128)S(6)} %select_n.18), dynamic_slice_sizes={1} | dynamic-slice | bytes 12 | tf_op jit(solution)/shard_map/dynamic_slice | solution.py:745
  15.4 0.0 collective-permute-done
  15.4 3.1 %collective-permute-done.1 = bf16[64,64]{1,0:T(8,128)(2,1)S(1)} collective-permute-done((bf16[64,64]{1,0:T(8,128)(2,1)S(1)}, bf16[64,64]{1,0:T(8,128)(2,1)S(1)}, u32[]{:S(2)}, u32[]{:S(2)}) %collective-permute-start.1) | collective-permute-done | bytes 8224 | tf_op jit(solution)/shard_map/ppermute | solution.py:42
  18.5 1.0 %fusion.11 = (bf16[1,64,384]{2,1,0:T(8,128)(2,1)S(1)}, bf16[1,64,384]{2,1,0:T(8,128)(2,1)S(1)}) fusion(bf16[64,512]{1,0:T(8,128)(2,1)} %param.17, bf16[64,64]{1,0:T(8,128)(2,1)S(1)} %collective-permute-done, bf16[64,64]{1,0:T(8,128)(2,1)S(1)} %collective-permute-done.1), kind=kLoop, calls=%fused_computation.15 | loop fusion | flops 196608 | bytes 180224 | tf_op jit(solution)/shard_map/stack | solution.py:735
  19.5 1.4 %convolution_bitcast_fusion = f32[2,256,256]{2,1,0:T(8,128)S(1)} fusion(bf16[384,256,1]{1,0,2:T(8,128)(2,1)} %constant.56, bf16[1,64,384]{2,1,0:T(8,128)(2,1)S(1)} %get-tuple-element.9, bf16[1,64,384]{2,1,0:T(8,128)(2,1)S(1)} %get-tuple-element.8, bf16[256,256]{1,0:T(8,128)(2,1)} %constant.45.clone, s32[]{:T(128)S(6)} %select_n.16), kind=kOutput, calls=%fused_computation | convolution fusion | flops 42024960 | bytes 851972 | tf_op jit(solution)/shard_map/xc,jxd->jcd/dot_general | solution.py:741
  20.9 0.7 pad_maximum_fusion
  22.9 0.0 all-reduce.2.cloned.1.call-update
  23.5 0.0 copy-done
  23.6 0.5 constant_dynamic-slice_fusion.coef_ref
  24.1 37.6 %shard_map.176.own_hbm = bf16[24,128,256]{2,1,0:T(8,128)(2,1)} custom-call(f32[1,37]{1,0:T(1,128)} %constant_dynamic-slice_fusion.coef_ref, s32[2,512]{1,0:T(2,128)} %bitcast.18, f32[1,512]{1,0:T(1,128)} %bitcast.19, f32[38,88,128]{2,1,0:T(8,128)} %constant.47.clone.basis_hbm, f32[128,128]{1,0:T(8,128)} %constant.48.clone.cos_hbm, ...), custom_call_target="tpu_custom_call" | custom-call | flops 60000002048 | bytes 8000000 | tf_op jit(solution)/shard_map/pallas_call | solution.py:441
  61.7 0.0 all-reduce.2.cloned.1.call-done.spec_ref
  61.7 21.8 %shard_map.177 = (bf16[64,512]{1,0:T(8,128)(2,1)}, bf16[64,512]{1,0:T(8,128)(2,1)}) custom-call(bf16[24,128,256]{2,1,0:T(8,128)(2,1)} %shard_map.176.own_hbm, bf16[2,2,128,128]{3,2,1,0:T(8,128)(2,1)} %all-reduce.2.cloned.1.call-done.spec_ref, bf16[64,512]{1,0:T(8,128)(2,1)} %target_ref.1, f32[4,128,256]{2,1,0:T(8,128)} %constant.50.clone.turn_hbm, ...), custom_call_target="tpu_custom_call" | custom-call | flops 2000000000 | bytes 4000000 | tf_op jit(solution)/shard_map/pallas_call | solution.py:681
  83.5 1.5 %copy.24 = bf16[64,512]{1,0:T(8,128)(2,1)} copy(bf16[64,512]{1,0:T(8,128)(2,1)} %get-tuple-element.14) | data formatting | bytes 131072
  85.0 1.5 %copy.25 = bf16[64,512]{1,0:T(8,128)(2,1)} copy(bf16[64,512]{1,0:T(8,128)(2,1)} %get-tuple-element.15) | data formatting | bytes 131072
  (1 shorter events, 0.0 us)
Async XLA Ops:
  7.2 16.4 %copy-start = (f32[8,37]{1,0:T(8,128)S(1)}, f32[8,37]{1,0:T(8,128)}, u32[]{:S(2)}) copy-start(f32[8,37]{1,0:T(8,128)} %param.20) | copy-start | bytes 3556
  7.2 54.5 %all-reduce.2.cloned.1.call-start = ((), (), s32[]{:S(2)}) async-start(), calls=%async_computation | async-start | bytes 262144 | tf_op jit(solution)/shard_map/psum | solution.py:747
  8.0 7.4 %collective-permute-start = (bf16[64,64]{1,0:T(8,128)(2,1)S(1)}, bf16[64,64]{1,0:T(8,128)(2,1)S(1)}, u32[]{:S(2)}, u32[]{:S(2)}) collective-permute-start(bf16[64,64]{1,0:T(8,128)(2,1)S(1)} %get-tuple-element.10), channel_id=1, source_target_pairs={{0,1},{1,2},{2,3},{3,4},{4,5},{5,6},{6,7},{8,9},{9,10},{10,11},{11... | collective-permute-start | bytes 24584 | tf_op jit(solution)/shard_map/ppermute | solution.py:40
  12.9 5.6 %collective-permute-start.1 = (bf16[64,64]{1,0:T(8,128)(2,1)S(1)}, bf16[64,64]{1,0:T(8,128)(2,1)S(1)}, u32[]{:S(2)}, u32[]{:S(2)}) collective-permute-start(bf16[64,64]{1,0:T(8,128)(2,1)S(1)} %get-tuple-element.11), channel_id=1, source_target_pairs={{1,0},{2,1},{3,2},{4,3},{5,4},{6,5},{7,6},{9,8},{10,9},{11,10},{12... | collective-permute-start | bytes 24584 | tf_op jit(solution)/shard_map/ppermute | solution.py:42
Sparse Core Ops, SparseCore 0:
  23.0 32.6 all-reduce.1

commit v3 on v2

v3 whole, which is shorter than its diff:
```python
import functools
import math

import jax
import jax.numpy as jnp
import ml_dtypes
import numpy as np
from jax import lax
from jax.experimental import pallas as pl
from jax.experimental.pallas import tpu as pltpu
from jax.sharding import PartitionSpec as P

KB = 128
NR = 24
NZ = 37
RAD = 40
SHIFT = 24
HALO = 64
ITERS = 4
TS = 256
LAGS = 2 * SHIFT + 1
LP = 64
DISC = 88

STEEPNESS = 4.0
THRESHOLD = 0.5
RIDGE_SHARE = 0.001
F32 = jnp.float32
BF16 = jnp.bfloat16


def noll_terms(term_count):
    listing = []
    degree = 0
    while len(listing) < term_count:
        for azimuth in range(degree % 2, degree + 1, 2):
            if azimuth == 0:
                listing.append((degree, 0, 0))
            else:
                for repeat in range(2):
                    number = len(listing) + 1
                    listing.append((degree, azimuth, 2 if number % 2 == 0 else 1))
        degree += 1
    return listing[:term_count]


def radial_terms(degree, azimuth):
    powers = []
    for counter in range((degree - azimuth) // 2 + 1):
        factor = (
            (-1) ** counter
            * math.factorial(degree - counter)
            / (
                math.factorial(counter)
                * math.factorial((degree + azimuth) // 2 - counter)
                * math.factorial((degree - azimuth) // 2 - counter)
            )
        )
        powers.append((degree - 2 * counter, factor))
    return powers


@functools.lru_cache(None)
def zernike_table():
    u = (np.arange(DISC) - RAD)[:, None]
    v = (np.arange(KB) - RAD)[None, :]
    inside = (u * u + v * v <= RAD * RAD).astype(np.float64)
    rho = np.sqrt(u * u + v * v) / RAD
    theta = np.arctan2(v + 0.0 * u, u + 0.0 * v)
    planes = []
    for degree, azimuth, parity in noll_terms(NZ):
        radial = sum(f * rho**e for e, f in radial_terms(degree, azimuth))
        if azimuth == 0:
            plane = math.sqrt(degree + 1.0) * radial
        else:
            turn = np.cos if parity == 2 else np.sin
            plane = math.sqrt(2.0 * degree + 2.0) * radial * turn(azimuth * theta)
        planes.append(plane * inside)
    planes.append(inside)
    return np.stack(planes).astype(np.float32)


@functools.lru_cache(None)
def dft_tables():
    f = np.arange(KB)
    angle = 2.0 * np.pi / KB * ((f[:, None] * f[None, :]) % KB)
    return np.cos(angle).astype(np.float32), np.sin(angle).astype(np.float32)


def halves(x):
    high = x.astype(BF16)
    return high, (x - high.astype(F32)).astype(BF16)


def dot(x, y):
    return jnp.dot(x.astype(BF16), y.astype(BF16), preferred_element_type=F32)


def nt_mul(x, y):
    xh, xl = halves(x)
    yh, yl = halves(y)
    dims = (((1,), (1,)), ((), ()))
    return (
        lax.dot_general(xh, yh, dims, preferred_element_type=F32)
        + lax.dot_general(xl, yh, dims, preferred_element_type=F32)
        + lax.dot_general(xh, yl, dims, preferred_element_type=F32)
    )


def small_mul(m, x):
    mh, ml = halves(m)
    xh, xl = halves(x)
    return (
        jnp.dot(mh, xh, preferred_element_type=F32)
        + jnp.dot(ml, xh, preferred_element_type=F32)
        + jnp.dot(mh, xl, preferred_element_type=F32)
    )


def exact_dot(x, y):
    xh, xl = halves(x)
    yh, yl = halves(y)
    return dot(xh, yh) + dot(xl, yh) + dot(xh, yl)


def lane_join(parts):
    return jnp.concatenate(parts, axis=1)


def row_join(parts):
    return jnp.concatenate(parts, axis=0)


def eliminate(gram, floor):
    row = lax.broadcasted_iota(jnp.int32, (NR, KB), 0)
    lane = lax.broadcasted_iota(jnp.int32, (NR, KB), 1)
    aug = lane_join([gram, jnp.zeros((NR, KB - NR), F32)])
    aug = aug + jnp.where(lane == row + NR, 1.0, 0.0)
    scales = jnp.zeros((NR, KB), F32)
    block = 4
    for begin in range(0, NR, block):
        cols = [
            jnp.broadcast_to(aug[:, j : j + 1], (NR, KB)) for j in range(begin, begin + block)
        ]
        for m in range(block):
            j = begin + m
            pivot = cols[m][j : j + 1, :]
            good = pivot > floor
            safe = jnp.where(good, pivot, 1.0)
            inverse = jnp.where(good, 1.0 / safe, 0.0)
            root = jnp.where(good, lax.rsqrt(safe), 0.0)
            factor = jnp.where(row > j, cols[m] * inverse, 0.0)
            aug = aug - factor * aug[j : j + 1, :]
            for later in range(m + 1, block):
                cols[later] = cols[later] - factor * cols[later][j : j + 1, :]
            scales = jnp.where(row == j, root, scales)
    return aug * scales


GROUP = 8


@functools.lru_cache(None)
def phase_tables():
    frequency = np.arange(KB) - KB // 2

    def make(period):
        angle = 2.0 * np.pi / period * np.mod(np.arange(period)[:, None] * frequency, period)
        return [
            turn(angle.astype(np.float32)).astype(ml_dtypes.bfloat16) for turn in (np.cos, np.sin)
        ]

    return make(TS) + make(TS + 2 * HALO)


@functools.lru_cache(None)
def imaging_tables(group):
    cosine, sine, column_cos, column_sin = [t.astype(np.float32) for t in phase_tables()]
    rows = TS // group
    turns, backs = [], []
    for rank in range(group):
        c, s = [t[rank * rows : (rank + 1) * rows] for t in (cosine, sine)]
        turns.append(np.block([[c, -s], [s, c]]))
        backs.append(np.block([[c.T, -s.T], [s.T, c.T]]))
    inner = slice(HALO, HALO + TS)
    inverse = np.concatenate([column_cos[inner], -column_sin[inner]], axis=1).T
    adjoint = np.concatenate([column_cos[inner], column_sin[inner]], axis=1)
    spread = np.concatenate([column_cos, -column_sin], axis=1).T
    return tuple(
        np.ascontiguousarray(t) for t in (np.stack(turns), np.stack(backs), inverse, adjoint, spread)
    )


def whole_kernel(
    slit_ref, zern_ref, points_ref, weight_ref, mask_ref, target_ref,
    basis_hbm, cos_hbm, sin_hbm, block_hbm, back_hbm, spread_hbm, turn_hbm, inverse_hbm, adjoint_hbm,
    resist_ref, grad_ref,
    basis_ref, cos_ref, sin_ref, block_ref, back32_ref, spread32, turn32, inverse32, adjoint32,
    full, full_back, lag, lag_back,
    y_ref, z_ref, power_ref, pre_ref, pim_ref, edge_ref,
    held, wave_ref, field_ref, part_ref, got_ref, spart_ref, sgot_ref,
    acc_ref, rim_ref, left_ref, right_ref, mask_left, mask_right,
    local_sems, k_send, k_recv, g_send, g_recv, s_send, s_recv, r_send, r_recv, h_send, h_recv,
    *, group, line, tiles, rows, scale,
):
    rank, me = lax.axis_index("src"), lax.axis_index("tile")
    place = lax.rem(rank, tiles)
    right = lax.rem(me + 1, line)
    left = lax.rem(me + line - 1, line)
    peers = [lax.rem(rank + step, group) for step in range(1, group)]
    barrier = pltpu.get_barrier_semaphore()
    for peer in peers:
        pl.semaphore_signal(
            barrier, inc=1, device_id=(peer, me), device_id_type=pl.DeviceIdType.MESH
        )
    for side in (left, right):
        pl.semaphore_signal(
            barrier, inc=1, device_id=(rank, side), device_id_type=pl.DeviceIdType.MESH
        )
    loads = [
        (basis_hbm, basis_ref), (cos_hbm, cos_ref), (sin_hbm, sin_ref), (block_hbm, block_ref),
        (back_hbm.at[rank], back32_ref), (spread_hbm, spread32), (turn_hbm.at[rank], turn32),
        (inverse_hbm, inverse32), (adjoint_hbm, adjoint32),
    ]
    copies = [pltpu.make_async_copy(a, b, local_sems.at[i]) for i, (a, b) in enumerate(loads)]
    for copy in copies:
        copy.start()
    width = tiles * TS

    def send(src, dst, send_sem, recv_sem, device):
        copy = pltpu.make_async_remote_copy(
            src_ref=src, dst_ref=dst, send_sem=send_sem, recv_sem=recv_sem,
            device_id=device, device_id_type=pl.DeviceIdType.MESH,
        )
        copy.start()
        return copy

    halo_copies, spectrum_copies, kernel_copies = [], [], []

    def begin_exchange():
        pl.semaphore_wait(barrier, group - 1 + 2)
        ends = (mask_ref.at[:, width - 2 * HALO :], mask_ref.at[:, : 2 * HALO])
        halo_copies.append(send(ends[0], mask_left, h_send.at[0], h_recv.at[0], (rank, right)))
        halo_copies.append(send(ends[1], mask_right, h_send.at[1], h_recv.at[1], (rank, left)))

    def send_spectra():
        for copy in halo_copies:
            copy.wait_recv()
        for copy in copies[4:6]:
            copy.wait()
        spread = spread32[...].astype(BF16)
        back = back32_ref[...].astype(BF16)
        before = jnp.where(me > 0, mask_left[...].astype(F32), 0.0)
        after = jnp.where(me < line - 1, mask_right[...].astype(F32), 0.0)
        wide = lane_join([before, mask_ref[...].astype(F32), after])
        wide = pltpu.roll(wide, width + 3 * HALO, 1)
        for t in range(tiles):
            patch = wide[:, t * TS : (t + 1) * TS + 2 * HALO].astype(BF16)
            columns = lax.dot_general(
                patch, spread, (((1,), (1,)), ((), ())), preferred_element_type=F32
            ).astype(BF16)
            sums = dot(back, row_join([columns[:, :KB], -columns[:, KB:]]))
            spart_ref[t, 0] = sums[:KB].astype(BF16)
            spart_ref[t, 1] = (-sums[KB:]).astype(BF16)
        for step, peer in enumerate(peers):
            spectrum_copies.append(
                send(spart_ref, sgot_ref.at[step], s_send.at[step], s_recv.at[step], (peer, me))
            )

    lane = lax.broadcasted_iota(jnp.int32, (1, KB), 1)
    total = jnp.sum(weight_ref[...], axis=1, keepdims=True)
    weight = weight_ref[...] / (math.pi * RAD * RAD * total)
    px = SHIFT - points_ref[:, 0:1]
    py = SHIFT - points_ref[:, 1:2]
    lag_lane = lax.broadcasted_iota(jnp.int32, (points_ref.shape[0], KB), 1)
    hot_x = jnp.where(lag_lane == px, 1.0, 0.0).T[:LP]
    hot_y = jnp.where(jnp.where(lag_lane < LP, lag_lane, lag_lane - LP) == py, 1.0, 0.0)
    high, low = halves(hot_x * weight)
    omega = dot(high, hot_y) + dot(low, hot_y)
    omega_cat = lane_join([omega[i : i + 1] for i in range(LAGS)])
    begin_exchange()
    copies[0].wait()
    slit = slit_ref[place]
    waves = zern_ref[slit, 0] * basis_ref[0]
    for z in range(1, NZ):
        waves = waves + zern_ref[slit, z] * basis_ref[z]
    inside = basis_ref[NZ]
    angle = 2.0 * math.pi * waves
    pr = inside * jnp.cos(angle)
    pi = inside * jnp.sin(angle)
    p40 = (pr[80:81, 40:41], pi[80:81, 40:41])
    m40 = (pr[0:1, 40:41], pi[0:1, 40:41])
    q40 = (pr[40:41, 80:81], pi[40:41, 80:81])
    n40 = (pr[40:41, 0:1], pi[40:41, 0:1])
    for copy in copies[1:3]:
        copy.wait()
    c, s = cos_ref[...], sin_ref[...]
    full32 = row_join([lane_join([c, -s]), lane_join([s, c])])
    back32 = row_join([lane_join([c, s]), lane_join([-s, c])])
    full[...] = full32.astype(BF16)
    full_back[...] = back32.astype(BF16)
    keep_row = lax.broadcasted_iota(jnp.int32, (LP, KB), 0) < LAGS
    cy, sy = jnp.where(keep_row, c[:LP], 0.0), jnp.where(keep_row, s[:LP], 0.0)
    lag[...] = row_join([lane_join([cy, -sy]), lane_join([sy, cy])]).astype(BF16)
    keep_lane = lax.broadcasted_iota(jnp.int32, (KB, KB), 1) < LAGS
    ct, st = jnp.where(keep_lane, c, 0.0), jnp.where(keep_lane, s, 0.0)
    lag_back[...] = row_join(
        [ct + pltpu.roll(st, LP, 1), pltpu.roll(ct, LP, 1) - st]
    ).astype(BF16)
    pupil = row_join([lane_join([pr, pi]), jnp.zeros((KB - DISC, 2 * KB), F32)])
    half = exact_dot(pupil, full32)
    hat = exact_dot(back32, row_join([half[:, :KB], half[:, KB:]]))
    hat = (hat[:KB], hat[KB:])
    unit = 1.0 / (KB * KB)
    pre_ref[...] = unit * hat[0]
    pim_ref[...] = unit * hat[1]
    power_ref[...] = unit * (hat[0] * hat[0] + hat[1] * hat[1])
    send_spectra()

    def times(scalar, re, im, conj):
        a, b = scalar
        b = -b if conj else b
        return a * re - b * im, a * im + b * re

    def entries(shape, items):
        row = lax.broadcasted_iota(jnp.int32, shape, 0)
        col = lax.broadcasted_iota(jnp.int32, shape, 1)
        matrix = jnp.zeros(shape, F32)
        for i, j, value in items:
            matrix = matrix + jnp.where((row == i) & (col == j), value, 0.0)
        return matrix.astype(BF16)

    end = LAGS - 1
    qr, qi = q40
    ar, ai = times(n40, qr, qi, True)
    start_fix = entries(
        (2 * KB, KB),
        [(0, end, -qr), (KB, end, -qi), (0, LP + end, qi), (KB, LP + end, -qr)],
    )
    gram_fix = entries(
        (KB, KB),
        [
            (end, 0, -ar), (LP + end, 0, ai), (LP + end, LP, -ar), (end, LP, -ai),
            (end, end, -1.0), (0, end, -ar), (LP, end, -ai),
            (LP + end, LP + end, -1.0), (LP, LP + end, -ar), (0, LP + end, ai),
        ],
    )
    final_fix = entries(
        (KB, 2 * KB),
        [(end, 0, -qr), (LP + end, 0, qi), (end, KB, -qi), (LP + end, KB, -qr)],
    )

    copies[3].wait()

    def lanes_of(x, g):
        return x[:, g * KB : (g + 1) * KB]

    def stack(x, rows):
        x = x.astype(BF16)
        pieces = [x[g * rows : (g + 1) * rows] for g in range(GROUP)]
        return row_join(
            [lane_join([p[:, :KB] for p in pieces]), lane_join([p[:, KB:] for p in pieces])]
        )

    def unstack(x):
        x = x.astype(BF16)
        rows = x.shape[0] // 2
        return row_join(
            [lane_join([lanes_of(x[:rows], g), lanes_of(x[rows:], g)]) for g in range(GROUP)]
        )

    def scaled(x, re, im):
        tops, lows = [], []
        for g in range(GROUP):
            hr, hi = lanes_of(x[:KB], g), lanes_of(x[KB:], g)
            if im is None:
                tops.append((re * hr).astype(BF16))
                lows.append((re * hi).astype(BF16))
            else:
                tops.append((re * hr - im * hi).astype(BF16))
                lows.append((re * hi + im * hr).astype(BF16))
        return row_join([lane_join(tops), lane_join(lows)])

    def start(group, carry):
        base = group * GROUP
        xs = [
            lane_join([block_ref[0, base + g].astype(BF16), block_ref[1, base + g].astype(BF16)])
            for g in range(GROUP)
        ]
        two = dot(full_back[...], stack(dot(row_join(xs), full[...]), KB))
        three = dot(lag[...], scaled(two, pre_ref[...], -pim_ref[...]))
        rims = row_join([x.astype(F32)[40 : 40 + LP].astype(BF16) for x in xs])
        c = dot(lane_join([unstack(three), rims]), row_join([lag_back[...], start_fix]))
        z_ref[pl.ds(pl.multiple_of(base * LP, GROUP * LP), GROUP * LP), :] = c
        return carry

    lax.fori_loop(0, NR // GROUP, start, 0)
    at_first = pl.ds(0, NR, stride=LP)
    at_last = pl.ds(end, NR, stride=LP)
    within = lane < LAGS
    er = row_join([block_ref[0, k, 0:1, :] for k in range(NR)])
    ei = row_join([block_ref[1, k, 0:1, :] for k in range(NR)])
    er = jnp.where(within, pltpu.roll(er, KB - 40, 1), 0.0)
    ei = jnp.where(within, pltpu.roll(ei, KB - 40, 1), 0.0)
    er, ei = times(p40, er, ei, True)
    z_ref[at_last, :] = z_ref[at_last, :] - (er + pltpu.roll(ei, LP, 1))

    def load_cat(ref):
        return lane_join([ref[pl.ds(i, NR, stride=LP), :] for i in range(LAGS)])

    def store_cat(ref, value):
        for i in range(LAGS):
            ref[pl.ds(i, NR, stride=LP), :] = value[:, i * KB : (i + 1) * KB]

    y_ref[...] = jnp.zeros_like(y_ref)
    store_cat(y_ref, load_cat(z_ref) * omega_cat)

    def turned(scalar_a, scalar_b, value):
        cr, ci = times(scalar_a, scalar_b[0], scalar_b[1], True)
        return cr * value + jnp.where(lane < LP, -ci, ci) * pltpu.roll(value, LP, 1)

    def apply_gram():
        def body(group, carry):
            base = pl.multiple_of(group * GROUP * LP, GROUP * LP)
            at = pl.ds(base, GROUP * LP)
            y = y_ref[at, :].astype(BF16)
            two = dot(lag_back[...], stack(dot(y, lag[...]), LP))
            three = dot(lag[...], scaled(two, power_ref[...], None))
            z_ref[at, :] = dot(
                lane_join([unstack(three), y]), row_join([lag_back[...], gram_fix])
            )
            return carry

        lax.fori_loop(0, NR // GROUP, body, 0)
        y_first, y_last = y_ref[at_first, :], y_ref[at_last, :]
        z_ref[at_first, :] = z_ref[at_first, :] - turned(m40, p40, y_last)
        z_ref[at_last, :] = z_ref[at_last, :] - (y_last + turned(p40, m40, y_first))

    eye = lax.broadcasted_iota(jnp.int32, (NR, NR), 0) == lax.broadcasted_iota(
        jnp.int32, (NR, NR), 1
    )

    def trace_of(m):
        return jnp.sum(
            jnp.sum(jnp.where(eye, m, 0.0), axis=1, keepdims=True), axis=0, keepdims=True
        )

    for it in range(ITERS):
        apply_gram()
        yc, zc = load_cat(y_ref), load_cat(z_ref)
        gram = nt_mul(yc, zc)
        ridge = RIDGE_SHARE * trace_of(gram) / NR + 1e-06
        gram = gram + jnp.where(eye, ridge, 0.0)
        inverse = eliminate(gram, 0.0)[:, NR : 2 * NR]
        projected = small_mul(inverse, zc)
        if it < ITERS - 1:
            store_cat(y_ref, projected * omega_cat)
        else:
            mixing = nt_mul(projected * omega_cat, projected)
            upper = eliminate(mixing, 1e-6 * trace_of(mixing))[:, :NR]
            store_cat(y_ref, small_mul(small_mul(upper, inverse), yc))

    last = y_ref[at_last, :]
    er = pltpu.roll(jnp.where(lane < LP, last, 0.0), 40, 1)
    ei = pltpu.roll(jnp.where(lane < LP, 0.0, last), 40 + LP, 1)
    er, ei = times(p40, er, ei, False)
    edge_ref[...] = lane_join([er, ei])

    for group_index in range(NR // GROUP):
        base = group_index * GROUP
        y = y_ref[base * LP : (base + GROUP) * LP, :].astype(BF16)
        two = dot(lag_back[...], stack(dot(y, lag[...]), LP))
        three = dot(full[...], scaled(two, pre_ref[...], pim_ref[...]))
        a = dot(unstack(three), full_back[...])
        fix = dot(y, final_fix)
        edges = edge_ref[base : base + GROUP, :]
        for g in range(GROUP):
            top = g * KB
            head = a[top : top + 8]
            first_row = lax.broadcasted_iota(jnp.int32, head.shape, 0) == 0
            head = head - jnp.where(first_row, edges[g : g + 1], 0.0)
            held[0, base + g] = row_join(
                [
                    head,
                    a[top + 8 : top + 40],
                    a[top + 40 : top + 40 + LP] + fix[g * LP : (g + 1) * LP],
                    a[top + 40 + LP : top + KB],
                ]
            ).astype(BF16)
        span = pl.ds(base, GROUP)
        for step in range(1, tiles):
            kernel_copies.append(
                send(
                    held.at[0, span], held.at[step, span], k_send.at[step - 1, group_index],
                    k_recv.at[step - 1, group_index],
                    (rank - place + lax.rem(place + step, tiles), me),
                )
            )

    copies[6].wait()
    turn = turn32[...].astype(BF16)
    back = back32_ref[...].astype(BF16)
    spread = spread32[...].astype(BF16)
    for load in copies[7:]:
        load.wait()
    inverse = inverse32[...].astype(BF16)
    adjoint = adjoint32[...].astype(BF16)

    def parts(block):
        return block[:, :KB].astype(F32), block[:, KB:].astype(F32)

    for copy in spectrum_copies:
        copy.wait_recv()
    grad_copies = []
    for slot in range(tiles):
        t = lax.rem(place + tiles - slot, tiles)
        start = pl.multiple_of(t * TS, TS)
        if slot > 0:
            for copy in kernel_copies[slot - 1 :: tiles - 1]:
                copy.wait_recv()
        spectrum = spart_ref[t].astype(F32)
        for step in range(group - 1):
            spectrum = spectrum + sgot_ref[step, t].astype(F32)
        sre, sim = scale * spectrum[0], scale * spectrum[1]

        def forward(pair, carry):
            w = []
            for q in range(2):
                kr, ki = parts(held[slot, 2 * pair + q])
                w.append(((kr * sre + ki * sim).astype(BF16), (kr * sim - ki * sre).astype(BF16)))
            both = row_join([lane_join([w[0][h], w[1][h]]) for h in range(2)])
            turned = dot(turn, both).astype(BF16)
            for q in range(2):
                at = pl.ds(pl.multiple_of((2 * pair + q) * rows, rows), rows)
                lanes = slice(q * KB, (q + 1) * KB)
                wave_ref[at, :] = lane_join([turned[:rows, lanes], turned[rows:, lanes]])
            return carry

        lax.fori_loop(0, NR // 2, forward, 0, unroll=2)
        field_ref[...] = dot(wave_ref[...], inverse)

        def energy(k, total):
            field = field_ref[pl.ds(pl.multiple_of(k * rows, rows), rows), :]
            return total + field * field

        intensity = lax.fori_loop(0, NR, energy, jnp.zeros((rows, TS), F32), unroll=4)
        resist = 1.0 / (1.0 + jnp.exp(-STEEPNESS * (intensity - THRESHOLD)))
        goal = target_ref[:, pl.ds(start, TS)].astype(F32)
        resist_ref[:, pl.ds(start, TS)] = resist.astype(BF16)
        slope = 4.0 * (resist - goal) * STEEPNESS * resist * (1.0 - resist)

        def weigh(k, carry):
            at = pl.ds(pl.multiple_of(k * rows, rows), rows)
            wave_ref[at, :] = (field_ref[at, :] * slope).astype(BF16)
            return carry

        lax.fori_loop(0, NR, weigh, 0, unroll=4)
        wave_ref[...] = dot(wave_ref[...], adjoint).astype(BF16)

        def gather(pair, carry):
            acc_re, acc_im = carry
            waves = [
                wave_ref[pl.ds(pl.multiple_of((2 * pair + q) * rows, rows), rows), :]
                for q in range(2)
            ]
            both = row_join(
                [lane_join([waves[q][:, h * KB : (h + 1) * KB] for q in range(2)]) for h in range(2)]
            )
            turned = dot(back, both)
            for q in range(2):
                kr, ki = parts(held[slot, 2 * pair + q])
                tr = turned[:KB, q * KB : (q + 1) * KB]
                ti = turned[KB:, q * KB : (q + 1) * KB]
                acc_re = acc_re + kr * tr + ki * ti
                acc_im = acc_im + ki * tr - kr * ti
            return acc_re, acc_im

        zero = jnp.zeros((KB, KB), F32)
        acc_re, acc_im = lax.fori_loop(0, NR // 2, gather, (zero, zero), unroll=2)
        part_ref[slot, 0] = acc_re.astype(BF16)
        part_ref[slot, 1] = acc_im.astype(BF16)
        grad_copies.append(
            [
                send(
                    part_ref.at[slot], got_ref.at[slot, step], g_send.at[slot, step],
                    g_recv.at[slot, step], (peer, me),
                )
                for step, peer in enumerate(peers)
            ]
        )

    acc_ref[...] = jnp.zeros_like(acc_ref)
    for copies in grad_copies:
        for copy in copies:
            copy.wait_recv()
    for slot in range(tiles):
        t = lax.rem(place + tiles - slot, tiles)
        at = pl.ds(pl.multiple_of(t * TS, TS), TS + 2 * HALO)
        total = part_ref[slot].astype(F32)
        for step in range(1, group):
            total = total + got_ref[(slot - step) % tiles, step - 1].astype(F32)
        total = (scale * total).astype(BF16)
        rows_back = dot(turn, row_join([total[0], total[1]])).astype(BF16)
        patch = dot(lane_join([rows_back[:rows], rows_back[rows:]]), spread)
        acc_ref[:, at] = acc_ref[:, at] + patch

    lane = lax.broadcasted_iota(jnp.int32, (rows, 2 * HALO), 1)
    low = lane < HALO
    rim_ref[...] = jnp.where(
        low, acc_ref[:, : 2 * HALO], acc_ref[:, width : width + 2 * HALO]
    ).astype(BF16)
    rims = [
        send(rim_ref, left_ref, r_send.at[0], r_recv.at[0], (rank, right)),
        send(rim_ref, right_ref, r_send.at[1], r_recv.at[1], (rank, left)),
    ]
    inner = pltpu.roll(acc_ref[...], width + HALO, 1)[:, :width]
    rims[0].wait_recv()
    rims[1].wait_recv()
    from_left = pltpu.roll(left_ref[...].astype(F32), HALO, 1)
    from_right = pltpu.roll(right_ref[...].astype(F32), HALO, 1)
    from_left = jnp.where(low & (me > 0), from_left, 0.0)
    from_right = jnp.where((lane >= HALO) & (me < line - 1), from_right, 0.0)
    blocks = [
        inner[:, : 2 * HALO] + from_left,
        inner[:, 2 * HALO : width - 2 * HALO],
        inner[:, width - 2 * HALO :] + from_right,
    ]
    grad_ref[...] = lane_join(blocks).astype(BF16)
    for copy in halo_copies + spectrum_copies + kernel_copies + [c for copies in grad_copies for c in copies] + rims:
        copy.wait_send()


def on_device(mask, target, start_block, zernike, source_points, source_weight, tile_slit):
    tiles = tile_slit.shape[0]
    rows = mask.shape[0]
    group, line = lax.axis_size("src"), lax.axis_size("tile")
    scale = 1.0 / math.sqrt(TS * (TS + 2 * HALO))
    turns, backs, inverse, adjoint, spread = imaging_tables(group)
    cosine, sine = dft_tables()
    held = [
        jnp.asarray(t)
        for t in (zernike_table(), cosine, sine, start_block, backs, spread, turns, inverse, adjoint)
    ]
    vmem = pl.BlockSpec(memory_space=pltpu.VMEM)
    smem = pl.BlockSpec(memory_space=pltpu.SMEM)
    hbm = pl.BlockSpec(memory_space=pl.ANY)
    dma = pltpu.SemaphoreType.DMA
    own = [x.shape[1:] if x.shape[0] == group and x.ndim == 3 else x.shape for x in held]
    steps = group - 1
    scratch = [pltpu.VMEM(shape, F32) for shape in own]
    scratch += [
        pltpu.VMEM(shape, BF16)
        for shape in [(2 * KB, 2 * KB), (2 * KB, 2 * KB), (KB, 2 * KB), (2 * KB, KB)]
    ]
    scratch += [
        pltpu.VMEM(shape, F32)
        for shape in [(NR * LP, KB), (NR * LP, KB), (KB, KB), (KB, KB), (KB, KB), (NR, 2 * KB)]
    ]
    scratch += [
        pltpu.VMEM((tiles, NR, KB, 2 * KB), BF16),
        pltpu.VMEM((NR * rows, TS), BF16),
        pltpu.VMEM((NR * rows, TS), F32),
        pltpu.VMEM((tiles, 2, KB, KB), BF16),
        pltpu.VMEM((tiles, steps, 2, KB, KB), BF16),
        pltpu.VMEM((tiles, 2, KB, KB), BF16),
        pltpu.VMEM((steps, tiles, 2, KB, KB), BF16),
        pltpu.VMEM((rows, tiles * TS + 2 * HALO), F32),
    ]
    scratch += [pltpu.VMEM((rows, 2 * HALO), BF16)] * 5
    scratch += [
        dma((len(held),)), dma((tiles, NR // GROUP)), dma((tiles, NR // GROUP)),
        dma((tiles, steps)), dma((tiles, steps)), dma((steps,)), dma((steps,)),
        dma((2,)), dma((2,)), dma((2,)), dma((2,)),
    ]
    return pl.pallas_call(
        functools.partial(
            whole_kernel, group=group, line=line, tiles=tiles, rows=rows, scale=scale
        ),
        out_shape=(
            jax.ShapeDtypeStruct(target.shape, BF16),
            jax.ShapeDtypeStruct(target.shape, BF16),
        ),
        in_specs=[smem, smem] + [vmem] * 4 + [hbm] * len(held),
        out_specs=(vmem, vmem),
        scratch_shapes=scratch,
        compiler_params=pltpu.CompilerParams(
            vmem_limit_bytes=56 * 2**20, collective_id=0, has_side_effects=True
        ),
        cost_estimate=pl.CostEstimate(
            flops=8 * 10**9, bytes_accessed=8 * 10**6, transcendentals=0
        ),
    )(tile_slit, zernike, source_points, source_weight[None, :], mask, target, *held)


def solution(mesh):
    placed = (P("src", "tile"), P("src", "tile"), P(), P(), P(), P(), P("tile"))
    return jax.shard_map(
        on_device,
        mesh=mesh,
        in_specs=placed,
        out_specs=(P("src", "tile"), P("src", "tile")),
        check_vma=False,
    )
```

time: 93.7 us -> 68.3 us (0.73)
  between operations: 16.1 us -> 0.64 us
  starting transfers between devices: 6.16 us -> 0 us
  Pallas kernels: 59.4 us -> 63 us
  waiting for transfers between devices: 3.11 us -> 0 us
  other arithmetic: 1.66 us -> 0 us
  matrix products: 1.39 us -> 0 us
  local copies, waits for them, and re-layouts: 5.53 us -> 4.48 us
    ppermute x2 -> x0, starting transfers between devices: 6.12 us -> none  [the longest x1 4.83 us: with_halo(): lax.ppermute(tail, axis, [(i, (i + 1) % count) for i in range(ends)])]
    pallas_call x2 -> x1, Pallas kernels: 59.4 us -> 63 us  [on_device(): pl.pallas_call(functools.partial(whole_kernel, group=group, line=line, ti...]
    ppermute x2 -> x0, waiting for transfers between devices: 3.07 us -> none  [the longest x1 3.07 us: with_halo(): lax.ppermute(head, axis, [((i + 1) % count, i) for i in range(ends)])]
    dynamic_slice x2 -> x0, local copies, waits for them, and re-layouts: 1.76 us -> none  [the longest x1 1.24 us: on_device(): slit = lax.dynamic_slice_in_dim(tile_slit, rank % tiles_here, 1, 0)]
    another operation x3 -> x0, other arithmetic: 1.66 us -> none  [the longest x1 0.97 us: on_device(): jnp.stack([extended[:, counter * TS:counter * TS + patch_width] for count...]
    unnamed x4 -> x3, local copies, waits for them, and re-layouts: 2.96 us -> 4.48 us
    dot_general x1 -> x0, matrix products: 1.39 us -> none  [on_device(): jnp.einsum('xc,jxd->jcd', row_table, columns, preferred_element_type=jnp....]
  transfers between devices with their start and end apart: 3 -> 0, of which waited for: 1 -> 0; matrix products, arithmetic and copies ran while one was open for 2% -> 0% of each run, Pallas kernels for 40% -> 0%
where the time goes in v3:
time: 68.3 us; the launch traced here: 68.1 us
  Pallas kernels  63 us (92%)
  local copies, waits for them, and re-layouts  4.48 us (7%)
    pallas_call x1, Pallas kernels, on_device(): pl.pallas_call(functools.partial(whole_kernel, group=group, line=line, ti...  63 us
    unnamed x3, local copies, waits for them, and re-layouts  4.48 us

profile of v3, /device:TPU:0, one launch (start us, length us, event | category | flops | bytes accessed | tf_op | source)
XLA Modules:
  0.0 68.1 jit_solution(14425287041757070409)
XLA Ops:
  0.6 1.5 %copy.17.points_ref = s32[512,2]{1,0:T(8,128)} copy(s32[512,2]{0,1:T(2,128)} %param.19) | data formatting | bytes 8192 | tf_op args[4]
  2.2 63.0 %shard_map.158 = (bf16[64,512]{1,0:T(8,128)(2,1)}, bf16[64,512]{1,0:T(8,128)(2,1)}) custom-call(s32[2]{0:T(128)} %slit_ref.1, f32[8,37]{1,0:T(8,128)} %zern_ref.1, s32[512,2]{1,0:T(8,128)} %copy.17.points_ref, f32[1,512]{1,0:T(1,128)} %bitcast.1, bf16[64,512]{1,0:T(8,128)(2,1)} %mask_ref.1, bf16[64,512]{1,0:T(8,128)(2,1)} %target_ref.1, ...), custom_call_target="tpu_custom_call" | custom-call | flops 8000000000 | bytes 8000000 | tf_op jit(solution)/shard_map/pallas_call | solution.py:675
  65.1 1.5 %copy.20 = bf16[64,512]{1,0:T(8,128)(2,1)} copy(bf16[64,512]{1,0:T(8,128)(2,1)} %get-tuple-element.4) | data formatting | bytes 131072
  66.6 1.5 %copy.21 = bf16[64,512]{1,0:T(8,128)(2,1)} copy(bf16[64,512]{1,0:T(8,128)(2,1)} %get-tuple-element.5) | data formatting | bytes 131072

commit v4 on v3

--- a/solution.py
+++ b/solution.py
@@ -96,25 +96,23 @@
     return jnp.dot(x.astype(BF16), y.astype(BF16), preferred_element_type=F32)
 
 
+def split(x):
+    high = x.astype(BF16).astype(F32)
+    return high, x - high
+
+
 def nt_mul(x, y):
-    xh, xl = halves(x)
-    yh, yl = halves(y)
-    dims = (((1,), (1,)), ((), ()))
-    return (
-        lax.dot_general(xh, yh, dims, preferred_element_type=F32)
-        + lax.dot_general(xl, yh, dims, preferred_element_type=F32)
-        + lax.dot_general(xh, yl, dims, preferred_element_type=F32)
-    )
+    n, m = x.shape[0], y.shape[0]
+    left = jnp.concatenate(split(x), axis=0).astype(BF16)
+    right = jnp.concatenate(split(y), axis=0).astype(BF16)
+    out = lax.dot_general(left, right, (((1,), (1,)), ((), ())), preferred_element_type=F32)
+    return out[:n, :m] + out[n:, :m] + out[:n, m:]
 
 
 def small_mul(m, x):
-    mh, ml = halves(m)
-    xh, xl = halves(x)
-    return (
-        jnp.dot(mh, xh, preferred_element_type=F32)
-        + jnp.dot(ml, xh, preferred_element_type=F32)
-        + jnp.dot(mh, xl, preferred_element_type=F32)
-    )
+    mh, ml = split(m)
+    xh, xl = split(x)
+    return dot(lane_join([mh, mh, ml]), row_join([xh, xl, xh]))
 
 
 def exact_dot(x, y):
@@ -145,14 +143,11 @@
         for m in range(block):
             j = begin + m
             pivot = cols[m][j : j + 1, :]
-            good = pivot > floor
-            safe = jnp.where(good, pivot, 1.0)
-            inverse = jnp.where(good, 1.0 / safe, 0.0)
-            root = jnp.where(good, lax.rsqrt(safe), 0.0)
-            factor = jnp.where(row > j, cols[m] * inverse, 0.0)
-            aug = aug - factor * aug[j : j + 1, :]
+            root = jnp.where(pivot > floor, lax.rsqrt(jnp.maximum(pivot, 1e-30)), 0.0)
+            factor = jnp.where(row > j, cols[m] * root, 0.0)
+            aug = aug - factor * (aug[j : j + 1, :] * root)
             for later in range(m + 1, block):
-                cols[later] = cols[later] - factor * cols[later][j : j + 1, :]
+                cols[later] = cols[later] - factor * (cols[later][j : j + 1, :] * root)
             scales = jnp.where(row == j, root, scales)
     return aug * scales
 
@@ -194,7 +189,7 @@
 def whole_kernel(
     slit_ref, zern_ref, points_ref, weight_ref, mask_ref, target_ref,
     basis_hbm, cos_hbm, sin_hbm, block_hbm, back_hbm, spread_hbm, turn_hbm, inverse_hbm, adjoint_hbm,
-    resist_ref, grad_ref,
+    out_ref,
     basis_ref, cos_ref, sin_ref, block_ref, back32_ref, spread32, turn32, inverse32, adjoint32,
     full, full_back, lag, lag_back,
     y_ref, z_ref, power_ref, pre_ref, pim_ref, edge_ref,
@@ -270,13 +265,13 @@
     lane = lax.broadcasted_iota(jnp.int32, (1, KB), 1)
     total = jnp.sum(weight_ref[...], axis=1, keepdims=True)
     weight = weight_ref[...] / (math.pi * RAD * RAD * total)
-    px = SHIFT - points_ref[:, 0:1]
-    py = SHIFT - points_ref[:, 1:2]
-    lag_lane = lax.broadcasted_iota(jnp.int32, (points_ref.shape[0], KB), 1)
-    hot_x = jnp.where(lag_lane == px, 1.0, 0.0).T[:LP]
+    px = SHIFT - points_ref[0:1, :]
+    py = SHIFT - points_ref[1:2, :]
+    count = points_ref.shape[1]
+    hot_x = jnp.where(lax.broadcasted_iota(jnp.int32, (LP, count), 0) == px, weight, 0.0)
+    lag_lane = lax.broadcasted_iota(jnp.int32, (KB, count), 0)
     hot_y = jnp.where(jnp.where(lag_lane < LP, lag_lane, lag_lane - LP) == py, 1.0, 0.0)
-    high, low = halves(hot_x * weight)
-    omega = dot(high, hot_y) + dot(low, hot_y)
+    omega = nt_mul(hot_x, hot_y)
     omega_cat = lane_join([omega[i : i + 1] for i in range(LAGS)])
     begin_exchange()
     copies[0].wait()
@@ -431,7 +426,7 @@
             )
             return carry
 
-        lax.fori_loop(0, NR // GROUP, body, 0)
+        lax.fori_loop(0, NR // GROUP, body, 0, unroll=True)
         y_first, y_last = y_ref[at_first, :], y_ref[at_last, :]
         z_ref[at_first, :] = z_ref[at_first, :] - turned(m40, p40, y_last)
         z_ref[at_last, :] = z_ref[at_last, :] - (y_last + turned(p40, m40, y_first))
@@ -536,7 +531,7 @@
                 wave_ref[at, :] = lane_join([turned[:rows, lanes], turned[rows:, lanes]])
             return carry
 
-        lax.fori_loop(0, NR // 2, forward, 0, unroll=2)
+        lax.fori_loop(0, NR // 2, forward, 0, unroll=4)
         field_ref[...] = dot(wave_ref[...], inverse)
 
         def energy(k, total):
@@ -546,7 +541,7 @@
         intensity = lax.fori_loop(0, NR, energy, jnp.zeros((rows, TS), F32), unroll=4)
         resist = 1.0 / (1.0 + jnp.exp(-STEEPNESS * (intensity - THRESHOLD)))
         goal = target_ref[:, pl.ds(start, TS)].astype(F32)
-        resist_ref[:, pl.ds(start, TS)] = resist.astype(BF16)
+        out_ref[0, :, pl.ds(start, TS)] = resist.astype(BF16)
         slope = 4.0 * (resist - goal) * STEEPNESS * resist * (1.0 - resist)
 
         def weigh(k, carry):
@@ -576,7 +571,7 @@
             return acc_re, acc_im
 
         zero = jnp.zeros((KB, KB), F32)
-        acc_re, acc_im = lax.fori_loop(0, NR // 2, gather, (zero, zero), unroll=2)
+        acc_re, acc_im = lax.fori_loop(0, NR // 2, gather, (zero, zero), unroll=4)
         part_ref[slot, 0] = acc_re.astype(BF16)
         part_ref[slot, 1] = acc_im.astype(BF16)
         grad_copies.append(
@@ -625,7 +620,7 @@
         inner[:, 2 * HALO : width - 2 * HALO],
         inner[:, width - 2 * HALO :] + from_right,
     ]
-    grad_ref[...] = lane_join(blocks).astype(BF16)
+    out_ref[1] = lane_join(blocks).astype(BF16)
     for copy in halo_copies + spectrum_copies + kernel_copies + [c for copies in grad_copies for c in copies] + rims:
         copy.wait_send()
 
@@ -672,16 +667,13 @@
         dma((tiles, steps)), dma((tiles, steps)), dma((steps,)), dma((steps,)),
         dma((2,)), dma((2,)), dma((2,)), dma((2,)),
     ]
-    return pl.pallas_call(
+    out = pl.pallas_call(
         functools.partial(
             whole_kernel, group=group, line=line, tiles=tiles, rows=rows, scale=scale
         ),
-        out_shape=(
-            jax.ShapeDtypeStruct(target.shape, BF16),
-            jax.ShapeDtypeStruct(target.shape, BF16),
-        ),
+        out_shape=jax.ShapeDtypeStruct((2,) + target.shape, BF16),
         in_specs=[smem, smem] + [vmem] * 4 + [hbm] * len(held),
-        out_specs=(vmem, vmem),
+        out_specs=vmem,
         scratch_shapes=scratch,
         compiler_params=pltpu.CompilerParams(
             vmem_limit_bytes=56 * 2**20, collective_id=0, has_side_effects=True
@@ -689,7 +681,8 @@
         cost_estimate=pl.CostEstimate(
             flops=8 * 10**9, bytes_accessed=8 * 10**6, transcendentals=0
         ),
-    )(tile_slit, zernike, source_points, source_weight[None, :], mask, target, *held)
+    )(tile_slit, zernike, source_points.T, source_weight[None, :], mask, target, *held)
+    return out[0], out[1]
 
 
 def solution(mesh):

time: 68.3 us -> 56.6 us (0.83)
  Pallas kernels: 63 us -> 54.2 us
  local copies, waits for them, and re-layouts: 4.48 us -> 1.53 us
    pallas_call x1, Pallas kernels: 63 us -> 54.2 us  [on_device(): pl.pallas_call(functools.partial(whole_kernel, group=group, line=line, ti...]
    unnamed x3 -> x0, local copies, waits for them, and re-layouts: 4.48 us -> none
    squeeze x0 -> x1, local copies, waits for them, and re-layouts: none -> 1.53 us  [on_device(): return (out[0], out[1])]
where the time goes in v4:
time: 56.6 us; the launch traced here: 56.4 us
  Pallas kernels  54.2 us (96%)
  local copies, waits for them, and re-layouts  1.53 us (3%)
  between operations  0.64 us (1%)
    pallas_call x1, Pallas kernels, on_device(): pl.pallas_call(functools.partial(whole_kernel, group=group, line=line, ti...  54.2 us
    squeeze x1, local copies, waits for them, and re-layouts, on_device(): return (out[0], out[1])  1.53 us

profile of v4, /device:TPU:0, one launch (start us, length us, event | category | flops | bytes accessed | tf_op | source)
XLA Modules:
  0.0 56.4 jit_solution(9654854660259940271)
XLA Ops:
  0.6 54.2 %shard_map.158 = bf16[2,64,512]{2,1,0:T(8,128)(2,1)} custom-call(s32[2]{0:T(128)} %slit_ref.1, f32[8,37]{1,0:T(8,128)} %zern_ref.1, s32[2,512]{1,0:T(2,128)} %bitcast.6, f32[1,512]{1,0:T(1,128)} %bitcast.7, bf16[64,512]{1,0:T(8,128)(2,1)} %mask_ref.1, bf16[64,512]{1,0:T(8,128)(2,1)} %target_ref.1, f32[38,88,128]{2,1,0:T(8,128)} %constant.16.clone.basis_hbm, ...), custom_call_target="tpu_custom_call" | custom-call | flops 8000000000 | bytes 8000000 | tf_op jit(solution)/shard_map/pallas_call | solution.py:670
  54.9 1.5 %slice_bitcast_fusion = (bf16[64,512]{1,0:T(8,128)(2,1)}, bf16[64,512]{1,0:T(8,128)(2,1)}) fusion(bf16[2,64,512]{2,1,0:T(8,128)(2,1)} %shard_map.158), kind=kLoop, calls=%fused_computation | loop fusion | bytes 262144 | tf_op jit(solution)/shard_map/squeeze | solution.py:685

commit v5 on v4

--- a/solution.py
+++ b/solution.py
@@ -135,7 +135,7 @@
     aug = lane_join([gram, jnp.zeros((NR, KB - NR), F32)])
     aug = aug + jnp.where(lane == row + NR, 1.0, 0.0)
     scales = jnp.zeros((NR, KB), F32)
-    block = 4
+    block = 8
     for begin in range(0, NR, block):
         cols = [
             jnp.broadcast_to(aug[:, j : j + 1], (NR, KB)) for j in range(begin, begin + block)
@@ -389,7 +389,7 @@
         z_ref[pl.ds(pl.multiple_of(base * LP, GROUP * LP), GROUP * LP), :] = c
         return carry
 
-    lax.fori_loop(0, NR // GROUP, start, 0)
+    lax.fori_loop(0, NR // GROUP, start, 0, unroll=True)
     at_first = pl.ds(0, NR, stride=LP)
     at_last = pl.ds(end, NR, stride=LP)
     within = lane < LAGS

time: 56.6 us -> 54.9 us (0.970)
  Pallas kernels: 54.2 us -> 52.5 us
    pallas_call x1, Pallas kernels: 54.2 us -> 52.5 us  [on_device(): pl.pallas_call(functools.partial(whole_kernel, group=group, line=line, ti...]
where the time goes in v5:
time: 54.9 us; the launch traced here: 54.7 us
  Pallas kernels  52.5 us (96%)
  local copies, waits for them, and re-layouts  1.53 us (3%)
  between operations  0.64 us (1%)
    pallas_call x1, Pallas kernels, on_device(): pl.pallas_call(functools.partial(whole_kernel, group=group, line=line, ti...  52.5 us
    squeeze x1, local copies, waits for them, and re-layouts, on_device(): return (out[0], out[1])  1.53 us

profile of v5, /device:TPU:0, one launch (start us, length us, event | category | flops | bytes accessed | tf_op | source)
XLA Modules:
  0.0 54.7 jit_solution(12698146093430145022)
XLA Ops:
  0.6 52.5 %shard_map.158 = bf16[2,64,512]{2,1,0:T(8,128)(2,1)} custom-call(s32[2]{0:T(128)} %slit_ref.1, f32[8,37]{1,0:T(8,128)} %zern_ref.1, s32[2,512]{1,0:T(2,128)} %bitcast.6, f32[1,512]{1,0:T(1,128)} %bitcast.7, bf16[64,512]{1,0:T(8,128)(2,1)} %mask_ref.1, bf16[64,512]{1,0:T(8,128)(2,1)} %target_ref.1, f32[38,88,128]{2,1,0:T(8,128)} %constant.16.clone.basis_hbm, ...), custom_call_target="tpu_custom_call" | custom-call | flops 8000000000 | bytes 8000000 | tf_op jit(solution)/shard_map/pallas_call | solution.py:670
  53.1 1.5 %slice_bitcast_fusion = (bf16[64,512]{1,0:T(8,128)(2,1)}, bf16[64,512]{1,0:T(8,128)(2,1)}) fusion(bf16[2,64,512]{2,1,0:T(8,128)(2,1)} %shard_map.158), kind=kLoop, calls=%fused_computation | loop fusion | bytes 262144 | tf_op jit(solution)/shard_map/squeeze | solution.py:685
